TPU v7x, 128 devices: a whole 4x4x4 slice. The times are simulated.
128 devices in a mesh: ves: 32 (over z, x, core), deg: 4 (over y).
Axes of the slice: x: 4, y: 4, z: 4, core: 2. Of those that a mesh axis runs over, the one named last changes fastest.
Arguments:
- adj_velocity: bfloat16 [4096, 3, 544], P(('ves', 'deg')), may hold values from -6 to 6
- jacobian: bfloat16 [4096, 544], P(('ves', 'deg')), may hold values from 0.5 to 2
- self_kernel: bfloat16 [544, 544], replicated, may hold values from -0.25 to 0.25
- near_kernel_up: bfloat16 [544, 2112], replicated, may hold values from -0.25 to 0.25
- near_kernel_down: bfloat16 [2112, 544], replicated, may hold values from -0.125 to 0.125
- radial: float32 [2112], replicated, may hold values from 0.2 to 3
- near_dist: float32 [4096, 8], P(('ves', 'deg')), may hold values from 0.3 to 4
- near_owner: int32 [4096, 8], P(('ves', 'deg')), may hold values from 0 to 127, all different within a row; in each aligned block of 32 rows (0 to 31, 32 to 63, ...) at most 3 rows name the same one
- near_local: int32 [4096, 8], P(('ves', 'deg')), may hold values from 0 to 31
- live_pairs: int32 [128], P(('ves', 'deg')), may hold values from 64 to 256, as said below
- analysis: float32 [544, 288], replicated, may hold values from -0.25 to 0.25
- blocks: float32 [16, 3, 3, 4096], P('deg', None, None, 'ves'), as said below
Outputs:
- adj_coefficients: float32 [3, 288, 4096], P(None, 'deg', 'ves')
Inputs may be any that keep to these rules, and one draw needn't show every extreme that they name: `near_owner`: each row names 8 different devices. Among the rows of one device's 32 vesicles no device is named more than 3 times, and some device is named exactly 3 times. `live_pairs`: each device has at least a quarter of its slots live, and some device has all 256 live. `blocks`: each 3 x 3 block is strictly diagonally dominant by rows, with positive diagonal.
All inputs are finite; a program needn't handle non-finite values.
Results may differ from a plain program's by a relative error of at most 0.0041.
Values may be sent and summed in bfloat16 or wider, within the bound.
No kernel may reach another device: no remote copies, remote signals or barrier semaphores. Data moves between devices by JAX's collectives and lax.ppermute only.
A program may use at most 64 MiB of HBM per device.

v0:
```python
import jax
import jax.numpy as jnp
import numpy as np
from jax import lax
from jax.sharding import PartitionSpec as P


def coefficient_slots(order):
    widths = []
    for position in range(order // 2):
        widths.append(2 * position + 3)
        widths.append(2 * (order - position) + 1)
    return np.repeat(np.arange(order), np.array(widths))


def solve_three(matrix, rhs):
    cofactor = [
        [
            matrix[1][1] * matrix[2][2] - matrix[1][2] * matrix[2][1],
            matrix[1][2] * matrix[2][0] - matrix[1][0] * matrix[2][2],
            matrix[1][0] * matrix[2][1] - matrix[1][1] * matrix[2][0],
        ],
        [
            matrix[0][2] * matrix[2][1] - matrix[0][1] * matrix[2][2],
            matrix[0][0] * matrix[2][2] - matrix[0][2] * matrix[2][0],
            matrix[0][1] * matrix[2][0] - matrix[0][0] * matrix[2][1],
        ],
        [
            matrix[0][1] * matrix[1][2] - matrix[0][2] * matrix[1][1],
            matrix[0][2] * matrix[1][0] - matrix[0][0] * matrix[1][2],
            matrix[0][0] * matrix[1][1] - matrix[0][1] * matrix[1][0],
        ],
    ]
    determinant = (
        matrix[0][0] * cofactor[0][0]
        + matrix[0][1] * cofactor[0][1]
        + matrix[0][2] * cofactor[0][2]
    )
    return jnp.stack(
        [
            (cofactor[0][col] * rhs[0] + cofactor[1][col] * rhs[1] + cofactor[2][col] * rhs[2])
            / determinant
            for col in range(3)
        ]
    )


def body(
    adj_velocity,
    jacobian,
    self_kernel,
    near_kernel_up,
    near_kernel_down,
    radial,
    near_dist,
    near_owner,
    near_local,
    live_pairs,
    analysis,
    blocks,
):
    ves_dev, comps, points = adj_velocity.shape
    near_slots = near_owner.shape[1]
    fine_points = near_kernel_up.shape[1]
    devices = lax.axis_size(("ves", "deg"))
    groups = lax.axis_size("deg")
    capacity = 3 * ves_dev * near_slots // (2 * devices)
    pair_rows = ves_dev * near_slots
    scaled = (adj_velocity.astype(jnp.float32) * jacobian.astype(jnp.float32)[:, None, :]).astype(
        jnp.bfloat16
    )
    self_term = jnp.dot(
        scaled.reshape(-1, points), self_kernel, preferred_element_type=jnp.float32
    ).reshape(ves_dev, comps, points)
    upsampled = jnp.dot(
        adj_velocity.reshape(-1, points), near_kernel_up, preferred_element_type=jnp.float32
    ).reshape(ves_dev, comps, fine_points)
    weights = 1.0 / (1.0 + near_dist[:, :, None] * radial[None, None, :])
    field = (upsampled[:, None] * weights[:, :, None]).astype(jnp.bfloat16)
    partials = jnp.dot(
        field.reshape(-1, fine_points), near_kernel_down, preferred_element_type=jnp.float32
    ).reshape(pair_rows, comps, points)
    width = partials.shape[2]
    live = jnp.arange(pair_rows, dtype=jnp.int32) < live_pairs[0]
    owners = near_owner.reshape(-1)
    onehot = (
        (owners[:, None] == jnp.arange(devices, dtype=jnp.int32)[None, :]) & live[:, None]
    ).astype(jnp.int32)
    ranks = jnp.sum(jnp.cumsum(onehot, axis=0) * onehot, axis=1) - 1
    slots = jnp.where(live, owners * capacity + ranks, devices * capacity)
    outgoing = (
        jnp.zeros((devices * capacity, comps, width), jnp.float32)
        .at[slots]
        .set(partials, mode="drop")
    )
    targets = (
        jnp.full((devices * capacity,), ves_dev, jnp.int32)
        .at[slots]
        .set(near_local.reshape(-1), mode="drop")
    )
    received, arrived = (
        lax.all_to_all(
            outgoing.reshape(devices, capacity, comps, width),
            ("ves", "deg"),
            split_axis=0,
            concat_axis=0,
            tiled=True,
        ),
        lax.all_to_all(
            targets.reshape(devices, capacity),
            ("ves", "deg"),
            split_axis=0,
            concat_axis=0,
            tiled=True,
        ),
    )
    near_sum = jax.ops.segment_sum(
        received.reshape(-1, comps, width), arrived.reshape(-1), num_segments=ves_dev + 1
    )[:ves_dev]
    coef = jnp.einsum(
        "vcp,pk->ckv", self_term + near_sum, analysis, precision=lax.Precision.HIGHEST
    )
    degree_major = lax.all_to_all(
        coef.astype(jnp.bfloat16), "deg", split_axis=1, concat_axis=2, tiled=True
    ).astype(jnp.float32)
    local_degrees = blocks.shape[0]
    group_coefs = degree_major.shape[1]
    table = jnp.asarray(coefficient_slots(local_degrees * groups), dtype=jnp.int32)
    group = lax.axis_index("deg")
    local_slots = (
        lax.dynamic_slice_in_dim(table, group * group_coefs, group_coefs) - group * local_degrees
    )
    select = (local_slots[:, None] == jnp.arange(local_degrees, dtype=jnp.int32)[None, :]).astype(
        jnp.float32
    )
    expanded = jnp.einsum("jd,dabv->abjv", select, blocks, precision=lax.Precision.HIGHEST)
    matrix = [[expanded[row, col] for col in range(3)] for row in range(3)]
    return solve_three(matrix, degree_major)


def solution(mesh):
    return jax.shard_map(
        body,
        mesh=mesh,
        in_specs=(
            P(("ves", "deg"), None, None),
            P(("ves", "deg"), None),
            P(),
            P(),
            P(),
            P(),
            P(("ves", "deg"), None),
            P(("ves", "deg"), None),
            P(("ves", "deg"), None),
            P(("ves", "deg")),
            P(),
            P("deg", None, None, "ves"),
        ),
        out_specs=P(None, "deg", "ves"),
        check_vma=False,
    )
```

profile of v0, /device:TPU:1, one launch (start us, length us, event | category | flops | bytes accessed | tf_op | source)
XLA Modules:
  0.0 181.9 jit_solution(7054589262361003277)
XLA Ops:
  0.0 0.9 copy.39
  0.9 0.1 eq.45
  1.0 0.1 eq.41
  1.1 0.7 broadcast_multiply_fusion
  2.5 0.1 copy.41
  2.6 0.3 fusion.11
  3.0 0.2 fusion.12
  3.3 0.1 copy.38
  3.3 0.1 mul.359
  3.4 0.8 copy.43
  4.2 0.1 reshape.519
  4.3 1.4 scatter_custom_fusion
  5.7 0.8 all_to_all.16
  6.5 11.5 %all-to-all-start = ((s32[128,1,3]{2,1,0:T(1,128)}), s32[128,1,3]{2,1,0:T(1,128)S(1)}, u32[]{:S(2)}, u32[]{:S(2)}) async-start(s32[128,1,3]{2,1,0:T(1,128)} %bitcast.14), calls=%async_computation | async-start | bytes 131072 | tf_op jit(solution)/shard_map/all_to_all | solution.py:109
  18.0 0.8 copy.45
  18.8 0.1 mul.363
  18.9 1.1 add_divide_fusion
  20.0 2.3 %fusion.6 = f32[32,3,2112]{2,0,1:T(8,128)S(1)} fusion(bf16[32,3,544]{2,0,1:T(8,128)(2,1)S(1)} %copy-done.2, bf16[544,2112]{1,0:T(8,128)(2,1)} %param.16), kind=kOutput, calls=%fused_computation.9 | convolution fusion | flops 220594176 | bytes 3213312 | tf_op jit(solution)/shard_map/dot_general | solution.py:75
  22.3 3.4 %fusion.1 = f32[256,3,544]{0,2,1:T(8,128)} fusion(f32[256,2112]{1,0:T(8,128)S(1)} %add_divide_fusion, f32[32,3,2112]{2,0,1:T(8,128)S(1)} %fusion.6, bf16[2112,544]{0,1:T(8,128)(2,1)S(1)} %copy-done), kind=kOutput, calls=%fused_computation.5 | convolution fusion | flops 1767997440 | bytes 6942720 | tf_op jit(solution)/shard_map/dot_general | solution.py:80
  25.7 3.7 %copy.47 = f32[256,3,544]{2,1,0:T(4,128)} copy(f32[256,3,544]{0,2,1:T(8,128)} %fusion.1) | data formatting | bytes 3342336 | tf_op jit(solution)/shard_map/dot_general | solution.py:80
  29.4 2.4 %broadcast_in_dim.13 = f32[384,3,544]{2,1,0:T(4,128)} broadcast(f32[]{:T(128)} %constant.8.clone.1), dimensions={} | broadcast | bytes 2506756 | tf_op jit(solution)/shard_map/broadcast_in_dim | solution.py:92
  31.8 30.6 %scatter_fusion = f32[384,3,544]{2,1,0:T(4,128)} fusion(f32[384,3,544]{2,1,0:T(4,128)} %broadcast_in_dim.13, s32[256]{0:T(256)S(1)} %bitcast.150, f32[256,3,544]{2,1,0:T(4,128)} %copy.47), kind=kCustom, calls=%fused_computation.1 | custom fusion | bytes 5014528 | tf_op jit(solution)/shard_map/scatter | solution.py:94
  62.3 5.0 %copy.49 = f32[128,3,3,544]{3,1,2,0:T(4,128)} copy(f32[128,3,3,544]{3,2,1,0:T(4,128)} %bitcast.138) | data formatting | bytes 5013504 | tf_op jit(solution)/shard_map/reshape | solution.py:103
  67.4 12.2 %all-to-all-start.1 = ((f32[128,3,3,544]{3,1,2,0:T(4,128)}), f32[128,3,3,544]{3,1,2,0:T(4,128)}, u32[]{:S(2)}, u32[]{:S(2)}) async-start(f32[128,3,3,544]{3,1,2,0:T(4,128)} %copy.49), calls=%async_computation.1 | async-start | bytes 7864320 | tf_op jit(solution)/shard_map/all_to_all | solution.py:102
  79.6 0.8 dynamic-slice_subtract_fusion
  80.3 0.5 broadcast.116
  80.9 0.8 reduce.3
  81.7 0.2 reshape.533
  81.9 47.8 %all-to-all-done.1 = f32[128,3,3,544]{3,1,2,0:T(4,128)} async-done(((f32[128,3,3,544]{3,1,2,0:T(4,128)}), f32[128,3,3,544]{3,1,2,0:T(4,128)}, u32[]{:S(2)}, u32[]{:S(2)}) %all-to-all-start.1) | async-done | bytes 2506784 | tf_op jit(solution)/shard_map/all_to_all | solution.py:102
  129.7 5.0 %copy.68 = f32[128,3,3,544]{3,2,1,0:T(4,128)} copy(f32[128,3,3,544]{3,1,2,0:T(4,128)} %all-to-all-done.1) | data formatting | bytes 5013504 | tf_op jit(solution)/shard_map/reshape | solution.py:118
  134.7 0.0 copy-start.1
  134.7 34.6 %scatter_fusion.1 = f32[33,3,544]{2,1,0:T(4,128)S(1)} fusion(f32[33,3,544]{2,1,0:T(4,128)S(1)} %broadcast_in_dim.9, s32[384]{0:T(512)S(1)} %reshape.533, f32[384,3,544]{2,1,0:T(4,128)} %bitcast.139), kind=kCustom, calls=%fused_computation.2 | custom fusion | flops 626688 | bytes 7521792 | tf_op jit(solution)/shard_map/scatter-add | solution.py:117
  169.3 0.1 slice.83
  169.4 1.4 convolution_add_fusion
  170.9 0.9 fusion.8
  171.8 0.2 copy.53
  172.0 0.9 reshape.556
  172.8 3.3 %all-to-all-start.2 = ((bf16[4,2,3456]{2,1,0:T(2,128)(2,1)}), bf16[4,2,3456]{2,1,0:T(2,128)(2,1)S(1)}, u32[]{:S(2)}, u32[]{:S(2)}) async-start(bf16[4,2,3456]{2,1,0:T(2,128)(2,1)} %reshape.556), calls=%async_computation.2 | async-start | bytes 110592 | tf_op jit(solution)/shard_map/all_to_all | solution.py:123
  176.1 0.4 convolution_bitcast_fusion
  176.5 4.0 %all-to-all-done.2 = bf16[4,2,3456]{2,1,0:T(2,128)(2,1)S(1)} async-done(((bf16[4,2,3456]{2,1,0:T(2,128)(2,1)}), bf16[4,2,3456]{2,1,0:T(2,128)(2,1)S(1)}, u32[]{:S(2)}, u32[]{:S(2)}) %all-to-all-start.2) | async-done | bytes 55328 | tf_op jit(solution)/shard_map/all_to_all | solution.py:123
  180.5 0.2 reshape.557
  180.7 0.2 copy.54
  180.9 0.1 copy.55
  181.0 0.1 copy.56
  181.1 0.1 copy.57
  181.1 0.1 add_divide_fusion.3
  181.2 0.1 add_divide_fusion.2
  181.3 0.7 pad_maximum_fusion
  (23 shorter events, 0.2 us)
Async XLA Ops:
  0.0 22.3 %copy-start = (bf16[2112,544]{0,1:T(8,128)(2,1)S(1)}, bf16[2112,544]{0,1:T(8,128)(2,1)}, u32[]{:S(2)}) copy-start(bf16[2112,544]{0,1:T(8,128)(2,1)} %param.17) | copy-start | bytes 6893572
  0.0 20.0 %copy-start.2 = (bf16[32,3,544]{2,0,1:T(8,128)(2,1)S(1)}, bf16[32,3,544]{2,0,1:T(8,128)(2,1)}, u32[]{:S(2)}) copy-start(bf16[32,3,544]{2,0,1:T(8,128)(2,1)} %param.13) | copy-start | bytes 313348
  6.5 60.8 %all-to-all-start = ((s32[128,1,3]{2,1,0:T(1,128)}), s32[128,1,3]{2,1,0:T(1,128)S(1)}, u32[]{:S(2)}, u32[]{:S(2)}) async-start(s32[128,1,3]{2,1,0:T(1,128)} %bitcast.14), calls=%async_computation | async-start | bytes 131072 | tf_op jit(solution)/shard_map/all_to_all | solution.py:109
  67.4 12.2 %copy-start.3 = (bf16[32,544]{1,0:T(8,128)(2,1)S(1)}, bf16[32,544]{1,0:T(8,128)(2,1)}, u32[]{:S(2)}) copy-start(bf16[32,544]{1,0:T(8,128)(2,1)} %param.14) | copy-start | bytes 104452
  67.4 62.3 %all-to-all-start.1 = ((f32[128,3,3,544]{3,1,2,0:T(4,128)}), f32[128,3,3,544]{3,1,2,0:T(4,128)}, u32[]{:S(2)}, u32[]{:S(2)}) async-start(f32[128,3,3,544]{3,1,2,0:T(4,128)} %copy.49), calls=%async_computation.1 | async-start | bytes 7864320 | tf_op jit(solution)/shard_map/all_to_all | solution.py:102
  134.7 36.1 %copy-start.1 = (f32[544,288]{0,1:T(8,128)S(1)}, f32[544,288]{0,1:T(8,128)}, u32[]{:S(2)}) copy-start(f32[544,288]{0,1:T(8,128)} %param.23) | copy-start | bytes 1880068
  169.3 6.8 %copy-start.4 = (f32[4,3,3,128]{3,0,2,1:T(4,128)S(1)}, f32[4,3,3,128]{3,0,2,1:T(4,128)}, u32[]{:S(2)}) copy-start(f32[4,3,3,128]{3,0,2,1:T(4,128)} %param.24) | copy-start | bytes 55300
  172.8 7.7 %all-to-all-start.2 = ((bf16[4,2,3456]{2,1,0:T(2,128)(2,1)}), bf16[4,2,3456]{2,1,0:T(2,128)(2,1)S(1)}, u32[]{:S(2)}, u32[]{:S(2)}) async-start(bf16[4,2,3456]{2,1,0:T(2,128)(2,1)} %reshape.556), calls=%async_computation.2 | async-start | bytes 110592 | tf_op jit(solution)/shard_map/all_to_all | solution.py:123
where the time goes:
time: 184 us; the launch traced here: 182 us
  local copies, waits for them, and re-layouts  54.5 us (30%)
  waiting for transfers between devices  51.8 us (28%)
  other arithmetic  39.3 us (21%)
  starting transfers between devices  26.9 us (15%)
  matrix products  8.39 us (5%)
    all_to_all x1, waiting for transfers between devices, body(): lax.all_to_all(outgoing.reshape(devices, capacity, comps, width), ('ves',...  47.8 us
    scatter-add x1, other arithmetic, body(): jax.ops.segment_sum(received.reshape(-1, comps, width), arrived.reshape(-...  34.6 us
    scatter x1, local copies, waits for them, and re-layouts, body(): outgoing = jnp.zeros((devices * capacity, comps, width), jnp.float32).at[...  30.6 us
    all_to_all x1, starting transfers between devices, body(): lax.all_to_all(outgoing.reshape(devices, capacity, comps, width), ('ves',...  12.2 us
    all_to_all x1, starting transfers between devices, body(): lax.all_to_all(targets.reshape(devices, capacity), ('ves', 'deg'), split_...  11.5 us
    reshape x1, local copies, waits for them, and re-layouts, body(): outgoing.reshape(devices, capacity, comps, width)  5.03 us
    reshape x1, local copies, waits for them, and re-layouts, body(): received.reshape(-1, comps, width)  5.02 us
    all_to_all x1, waiting for transfers between devices, body(): lax.all_to_all(coef.astype(jnp.bfloat16), 'deg', split_axis=1, concat_axi...  4.02 us
  transfers between devices with their start and end apart: 3, of which 2 were waited for; matrix products, arithmetic and copies ran while one was open for 29% of the time, Pallas kernels for 0%

commit v1 on v0

v1 whole, which is shorter than its diff:
```python
import functools

import jax
import jax.numpy as jnp
import numpy as np
from jax import lax
from jax.experimental import pallas as pl
from jax.experimental.pallas import tpu as pltpu
from jax.sharding import PartitionSpec as P

VMEM = pltpu.CompilerParams(vmem_limit_bytes=56 * 1024 * 1024)
LANES = 128
NN = (((1,), (0,)), ((), ()))
NT = (((1,), (1,)), ((), ()))
TN = (((0,), (0,)), ((), ()))


def mm(a, b, dims=NN):
    return lax.dot_general(a, b, dims, preferred_element_type=jnp.float32)


def split(x):
    high = x.astype(jnp.bfloat16)
    return high, (x - high.astype(jnp.float32)).astype(jnp.bfloat16)


def columns(x, count):
    return jnp.concatenate(
        [jnp.broadcast_to(x[:, v : v + 1], (x.shape[0], LANES)) for v in range(count)], axis=0
    )


def pairs_kernel(
    live_ref, adj_ref, up_ref, down_ref, radial_ref, dist_ref, owner_ref, local_ref, analysis_ref,
    out_ref, ups_ref, m_ref, field_ref,
):
    comps, ves, points = adj_ref.shape
    fine = up_ref.shape[1]
    near = dist_ref.shape[0]
    pairs = near * ves
    groups = out_ref.shape[1]
    coefs = analysis_ref.shape[0]
    wide = coefs // groups
    high, low = split(analysis_ref[...])
    m = mm(high, down_ref[...]) + mm(low, down_ref[...])
    m_ref[...] = jnp.zeros_like(m_ref)
    for g in range(groups):
        m_ref[g * LANES : g * LANES + wide, :] = m[g * wide : (g + 1) * wide].astype(jnp.bfloat16)
    for c in range(comps):
        ups_ref[c] = mm(adj_ref[c], up_ref[...])
    owner = owner_ref[...]
    order = lax.broadcasted_iota(jnp.int32, owner.shape, 1) * near + lax.broadcasted_iota(
        jnp.int32, owner.shape, 0
    )
    dest = jnp.where(order < live_ref[0], owner // groups, -1)
    ident = (owner % groups) * ves + local_ref[...]
    lane = lax.broadcasted_iota(jnp.int32, (pairs, LANES), 1)
    hot = (columns(dest, ves) == lane).astype(jnp.float32)
    earlier = (
        lax.broadcasted_iota(jnp.int32, (pairs, pairs), 0)
        > lax.broadcasted_iota(jnp.int32, (pairs, pairs), 1)
    ).astype(jnp.float32)
    counts = mm(earlier.astype(jnp.bfloat16), hot.astype(jnp.bfloat16))
    ones = jnp.ones((8, LANES), jnp.bfloat16)
    rank = mm(ones, (hot * counts).astype(jnp.bfloat16), NT)
    place = mm(ones, (hot * (lane + 1).astype(jnp.float32)).astype(jnp.bfloat16), NT)
    slot = ((place - 1.0) * 12.0 + rank)[:1]
    row = lax.broadcasted_iota(jnp.int32, (32, 24, pairs), 1)
    base = lax.broadcasted_iota(jnp.int32, (32, 24, pairs), 0) * 12
    tile, inner = row // 8, row % 8
    code = (base + jnp.where(tile == 2, 8 + inner % 4, inner)).reshape(768, pairs)
    upper = jnp.where(tile == 2, inner // 4, tile).reshape(768, pairs)
    match = code == slot.astype(jnp.int32)
    pick_low = jnp.where(match & (upper == 0), 1.0, 0.0).astype(jnp.bfloat16)
    pick_high = jnp.where(match & (upper == 1), 1.0, 0.0).astype(jnp.bfloat16)
    dist = columns(dist_ref[...], ves)
    for start in range(0, fine, LANES):
        size = min(LANES, fine - start)
        at = slice(start, start + size)
        weight = 1.0 / (1.0 + dist[:, :size] * radial_ref[:, at])
        for c in range(comps):
            ups = jnp.concatenate(
                [jnp.broadcast_to(ups_ref[c, v : v + 1, at], (near, size)) for v in range(ves)], axis=0
            )
            field_ref[c, :, at] = (ups * weight).astype(jnp.bfloat16)
    part = [mm(field_ref[c], m_ref[...], NT) for c in range(comps)]
    ids = columns(ident.astype(jnp.float32), ves)
    for g in range(groups):
        at = slice(g * LANES, (g + 1) * LANES)
        second = pltpu.roll(part[1][:, at], wide, 1)
        third = pltpu.roll(part[2][:, at], 2 * wide - LANES, 1)
        low_half = jnp.where(lane < wide, part[0][:, at], second)
        high_half = jnp.where(lane < 2 * wide - LANES, second, third)
        high_half = jnp.where(lane == LANES - 1, ids, high_half)
        sent = mm(pick_low, low_half.astype(jnp.bfloat16)) + mm(
            pick_high, high_half.astype(jnp.bfloat16)
        )
        out_ref[:, g] = sent.reshape(32, 24, LANES).astype(jnp.bfloat16)


def self_kernel_body(adj_ref, jac_ref, kernel_ref, analysis_ref, out_ref):
    comps = adj_ref.shape[0]
    high, low = split(analysis_ref[...])
    s = mm(high, kernel_ref[...], NT) + mm(low, kernel_ref[...], NT)
    s_high, s_low = split(s)
    jac = jac_ref[...].astype(jnp.float32)
    for c in range(comps):
        scaled = (adj_ref[c].astype(jnp.float32) * jac).astype(jnp.bfloat16)
        out_ref[c] = mm(scaled, s_high, NT) + mm(scaled, s_low, NT)


def solve_kernel(group_ref, got_ref, self_ref, blocks_ref, out_ref):
    senders, rows, lanes = got_ref.shape
    comps, wide, ves = out_ref.shape
    got = got_ref[...].astype(jnp.float32)
    lane = lax.broadcasted_iota(jnp.int32, (senders, 8, lanes), 2).astype(jnp.float32)
    row = lax.broadcasted_iota(jnp.int32, (senders, 8, lanes), 1)
    first = got[:, 8:16, lanes - 1 : lanes] == lane
    other = jnp.where(got[:, 16:24, lanes - 1 : lanes] == lane, 1.0, 0.0)
    first = jnp.where(first, 1.0, 0.0)
    shifted = pltpu.roll(other, 4, 1)
    zero = jnp.zeros_like(first)
    to_low = jnp.concatenate([first, zero, jnp.where(row < 4, shifted, 0.0)], axis=1)
    to_high = jnp.concatenate([zero, first, jnp.where(row < 4, 0.0, other)], axis=1)
    flat = got_ref[...].reshape(senders * rows, lanes)
    near_low = mm(flat, to_low.reshape(senders * rows, lanes).astype(jnp.bfloat16), TN)
    near_high = mm(flat, to_high.reshape(senders * rows, lanes).astype(jnp.bfloat16), TN)
    cut = 2 * wide - lanes
    near = [
        near_low[:wide],
        jnp.concatenate([near_low[wide:], near_high[:cut]], axis=0),
        near_high[cut : cut + wide],
    ]
    rhs = [(self_ref[c] + near[c]).astype(jnp.bfloat16).astype(jnp.float32) for c in range(comps)]
    group = group_ref[0]
    at = lax.broadcasted_iota(jnp.int32, (wide, ves), 0)
    half = wide // 2

    def spread(r, c):
        b = [jnp.broadcast_to(blocks_ref[r, c, d : d + 1, :], (wide, ves)) for d in range(4)]
        lower = jnp.where(at < 4 * group + 3, b[0], b[1])
        upper = jnp.where(at < 4 * group + 5 + half, b[2], b[3])
        return jnp.where(at < half, lower, upper)

    m = [[spread(r, c) for c in range(3)] for r in range(3)]
    for c, value in enumerate(solve_three(m, rhs)):
        out_ref[c] = value


def solve_three(matrix, rhs):
    cofactor = [
        [
            matrix[1][1] * matrix[2][2] - matrix[1][2] * matrix[2][1],
            matrix[1][2] * matrix[2][0] - matrix[1][0] * matrix[2][2],
            matrix[1][0] * matrix[2][1] - matrix[1][1] * matrix[2][0],
        ],
        [
            matrix[0][2] * matrix[2][1] - matrix[0][1] * matrix[2][2],
            matrix[0][0] * matrix[2][2] - matrix[0][2] * matrix[2][0],
            matrix[0][1] * matrix[2][0] - matrix[0][0] * matrix[2][1],
        ],
        [
            matrix[0][1] * matrix[1][2] - matrix[0][2] * matrix[1][1],
            matrix[0][2] * matrix[1][0] - matrix[0][0] * matrix[1][2],
            matrix[0][0] * matrix[1][1] - matrix[0][1] * matrix[1][0],
        ],
    ]
    determinant = (
        matrix[0][0] * cofactor[0][0]
        + matrix[0][1] * cofactor[0][1]
        + matrix[0][2] * cofactor[0][2]
    )
    return [
        (cofactor[0][col] * rhs[0] + cofactor[1][col] * rhs[1] + cofactor[2][col] * rhs[2])
        / determinant
        for col in range(3)
    ]


def call_pairs(live, adj, up, down, radial, dist, owner, local, analysis, **kw):
    comps, ves, _ = adj.shape
    fine = up.shape[1]
    vmem = pl.BlockSpec(memory_space=pltpu.VMEM)
    return pl.pallas_call(
        pairs_kernel,
        out_shape=jax.ShapeDtypeStruct((32, 4, 24, LANES), jnp.bfloat16),
        in_specs=[pl.BlockSpec(memory_space=pltpu.SMEM)] + [vmem] * 8,
        out_specs=vmem,
        scratch_shapes=[
            pltpu.VMEM((comps, ves, fine), jnp.float32),
            pltpu.VMEM((4 * LANES, fine), jnp.bfloat16),
            pltpu.VMEM((comps, ves * dist.shape[0], fine), jnp.bfloat16),
        ],
        compiler_params=VMEM,
        name="pairs",
        **kw,
    )(live, adj, up, down, radial, dist, owner, local, analysis)


def call_self(adj, jac, kernel, analysis, **kw):
    comps, ves, _ = adj.shape
    return pl.pallas_call(
        self_kernel_body,
        out_shape=jax.ShapeDtypeStruct((comps, ves, analysis.shape[0]), jnp.float32),
        compiler_params=VMEM,
        name="self_term",
        **kw,
    )(adj, jac, kernel, analysis)


def call_solve(group, got, self_term, blocks, **kw):
    vmem = pl.BlockSpec(memory_space=pltpu.VMEM)
    return pl.pallas_call(
        solve_kernel,
        out_shape=jax.ShapeDtypeStruct(self_term.shape, jnp.float32),
        in_specs=[pl.BlockSpec(memory_space=pltpu.SMEM)] + [vmem] * 3,
        out_specs=vmem,
        compiler_params=VMEM,
        name="solve",
        **kw,
    )(group, got, self_term, blocks)


def body(
    adj_velocity,
    jacobian,
    self_kernel,
    near_kernel_up,
    near_kernel_down,
    radial,
    near_dist,
    near_owner,
    near_local,
    live_pairs,
    analysis,
    blocks,
):
    ves_dev, comps, points = adj_velocity.shape
    groups = lax.axis_size("deg")
    coefs = analysis.shape[1]
    wide = coefs // groups
    adj = adj_velocity.transpose(1, 0, 2)
    down = near_kernel_down.T
    projection = analysis.T
    sent = call_pairs(
        live_pairs, adj, near_kernel_up, down, radial[None, :], near_dist.T, near_owner.T,
        near_local.T, projection,
    )
    got = lax.all_to_all(
        sent.reshape(128, 24, LANES), ("ves", "deg"), split_axis=0, concat_axis=0, tiled=True
    )
    group = lax.axis_index("deg")
    own = call_self(adj, jacobian, self_kernel, projection)
    own = own.reshape(comps, ves_dev, groups, wide).transpose(2, 0, 3, 1)
    parts = [lax.dynamic_index_in_dim(own, group, 0, keepdims=False)]
    for i in range(1, groups):
        block = lax.dynamic_index_in_dim(own, (group + i) % groups, 0, keepdims=False)
        parts.append(lax.ppermute(block, "deg", [(j, (j + i) % groups) for j in range(groups)]))
    stacked = jnp.stack(parts)
    order = (group - jnp.arange(groups)) % groups
    self_term = jnp.take(stacked, order, axis=0).transpose(1, 2, 0, 3).reshape(comps, wide, -1)
    return call_solve(group[None].astype(jnp.int32), got, self_term, blocks.transpose(1, 2, 0, 3))


def solution(mesh):
    return jax.shard_map(
        body,
        mesh=mesh,
        in_specs=(
            P(("ves", "deg"), None, None),
            P(("ves", "deg"), None),
            P(),
            P(),
            P(),
            P(),
            P(("ves", "deg"), None),
            P(("ves", "deg"), None),
            P(("ves", "deg"), None),
            P(("ves", "deg")),
            P(),
            P("deg", None, None, "ves"),
        ),
        out_specs=P(None, "deg", "ves"),
        check_vma=False,
    )
```

time: 184 us -> 43.9 us (0.24)
  local copies, waits for them, and re-layouts: 54.5 us -> 4.82 us
  waiting for transfers between devices: 51.8 us -> 6.24 us
  other arithmetic: 39.3 us -> 0.14 us
  Pallas kernels: 0 us -> 16.3 us
  starting transfers between devices: 26.9 us -> 15.3 us
  matrix products: 8.39 us -> 0 us
    all_to_all x3 -> x1, waiting for transfers between devices: 51.8 us -> 0.13 us  [body(): lax.all_to_all(sent.reshape(128, 24, LANES), ('ves', 'deg'), split_axis=0...]
    scatter-add x1 -> x0, other arithmetic: 34.6 us -> none  [body(): jax.ops.segment_sum(received.reshape(-1, comps, width), arrived.reshape(-...]
    scatter x2 -> x0, local copies, waits for them, and re-layouts: 32 us -> none  [the longest x1 30.6 us: body(): outgoing = jnp.zeros((devices * capacity, comps, width), jnp.float32).at[...]
    pallas_call x0 -> x3, Pallas kernels: none -> 16.3 us  [the longest x1 9.9 us: call_pairs(): pl.pallas_call(pairs_kernel, out_shape=jax.ShapeDtypeStruct((32, 4, 24, L...]
    all_to_all x3 -> x1, starting transfers between devices: 26.9 us -> 11.5 us  [body(): lax.all_to_all(sent.reshape(128, 24, LANES), ('ves', 'deg'), split_axis=0...]
    dot_general x5 -> x0, matrix products: 8.39 us -> none  [the longest x1 3.43 us: body(): jnp.dot(field.reshape(-1, fine_points), near_kernel_down, preferred_eleme...]
    reshape x3 -> x2, local copies, waits for them, and re-layouts: 10.1 us -> 1.82 us  [the longest x1 1.06 us: body(): own = own.reshape(comps, ves_dev, groups, wide).transpose(2, 0, 3, 1)]
    ppermute x0 -> x3, waiting for transfers between devices: none -> 6.11 us  [body(): lax.ppermute(block, 'deg', [(j, (j + i) % groups) for j in range(groups)])]
  transfers between devices with their start and end apart: 3 -> 4, of which waited for: 2 -> 4; matrix products, arithmetic and copies ran while one was open for 29% -> 6% of each run, Pallas kernels for 0% -> 9%
where the time goes in v1:
time: 43.9 us; the launch traced here: 43.6 us
  Pallas kernels  16.3 us (37%)
  starting transfers between devices  15.3 us (35%)
  waiting for transfers between devices  6.24 us (14%)
  local copies, waits for them, and re-layouts  4.82 us (11%)
  between operations  0.77 us (2%)
    all_to_all x1, starting transfers between devices, body(): lax.all_to_all(sent.reshape(128, 24, LANES), ('ves', 'deg'), split_axis=0...  11.5 us
    pallas_call x1, Pallas kernels, call_pairs(): pl.pallas_call(pairs_kernel, out_shape=jax.ShapeDtypeStruct((32, 4, 24, L...  9.9 us
    ppermute x3, waiting for transfers between devices, body(): lax.ppermute(block, 'deg', [(j, (j + i) % groups) for j in range(groups)])  6.11 us
    ppermute x3, starting transfers between devices, body(): lax.ppermute(block, 'deg', [(j, (j + i) % groups) for j in range(groups)])  3.83 us
    pallas_call x1, Pallas kernels, call_self(): pl.pallas_call(self_kernel_body, out_shape=jax.ShapeDtypeStruct((comps, v...  3.72 us
    pallas_call x1, Pallas kernels, call_solve(): pl.pallas_call(solve_kernel, out_shape=jax.ShapeDtypeStruct(self_term.sha...  2.68 us
    broadcast_in_dim x1, local copies, waits for them, and re-layouts, body(): radial[None, :]  1.31 us
    reshape x1, local copies, waits for them, and re-layouts, body(): own = own.reshape(comps, ves_dev, groups, wide).transpose(2, 0, 3, 1)  1.06 us
  transfers between devices with their start and end apart: 4, of which 4 were waited for; matrix products, arithmetic and copies ran while one was open for 6% of the time, Pallas kernels for 9%

profile of v1, /device:TPU:1, one launch (start us, length us, event | category | flops | bytes accessed | tf_op | source)
XLA Modules:
  0.0 43.6 jit_solution(2369674454175083610)
XLA Ops:
  0.7 1.3 %broadcast_in_dim.17.radial_ref = f32[1,2112]{1,0:T(1,128)} reshape(f32[2112]{0:T(1024)} %param.17) | data formatting | bytes 16896 | tf_op jit(solution)/shard_map/broadcast_in_dim | solution.py:246
  2.0 9.9 %pairs.1 = bf16[32,4,24,128]{3,2,1,0:T(8,128)(2,1)} custom-call(s32[1]{0:T(128)S(6)} %copy.26.live_ref, bf16[3,32,544]{2,1,0:T(8,128)(2,1)} %bitcast.40, bf16[544,2112]{1,0:T(8,128)(2,1)} %up_ref.1, bf16[544,2112]{1,0:T(8,128)(2,1)} %bitcast.38, f32[1,2112]{1,0:T(1,128)} %broadcast_in_dim.17.radial_ref, f32[8,32]{1,0:T(8,128)} %bitcast.50, ...), custom_call_target="tpu_custom_call" | custom-call | tf_op jit(solution)/shard_map/pairs/pallas_call | solution.py:184
  11.9 11.5 %all-to-all-start = ((bf16[128,24,128]{2,1,0:T(8,128)(2,1)}), bf16[128,24,128]{2,1,0:T(8,128)(2,1)S(1)}, u32[]{:S(2)}, u32[]{:S(2)}) async-start(bf16[128,24,128]{2,1,0:T(8,128)(2,1)} %bitcast.35), calls=%async_computation | async-start | bytes 1572864 | tf_op jit(solution)/shard_map/all_to_all | solution.py:249
  23.4 3.7 %self_term.1 = f32[3,32,288]{2,1,0:T(8,128)} custom-call(bf16[3,32,544]{2,1,0:T(8,128)(2,1)} %bitcast.41, bf16[32,544]{1,0:T(8,128)(2,1)} %jac_ref.1, bf16[544,544]{1,0:T(8,128)(2,1)} %kernel_ref.1, f32[288,544]{1,0:T(8,128)} %bitcast.37), custom_call_target="tpu_custom_call" | custom-call | tf_op jit(solution)/shard_map/self_term/pallas_call | solution.py:202
  27.1 1.1 %reshape.64 = f32[3,32,4,72]{3,2,1,0:T(4,128)S(1)} reshape(f32[3,32,288]{2,1,0:T(8,128)} %self_term.1) | data formatting | bytes 221184 | tf_op jit(solution)/shard_map/reshape | solution.py:254
  28.2 0.2 constant_dynamic-slice_fusion.3
  28.4 2.7 %collective-permute-start.2 = (f32[3,72,32]{1,2,0:T(8,128)S(1)}, f32[3,72,32]{1,2,0:T(8,128)S(1)}, u32[]{:S(2)}, u32[]{:S(2)}) collective-permute-start(f32[3,72,32]{1,2,0:T(8,128)S(1)} %bitcast.46), channel_id=1, source_target_pairs={{0,3},{1,0},{2,1},{3,2},{4,7},{5,4},{6,5},{7,6},{8,11},{9,8},{10,9... | collective-permute-start | bytes 82952 | tf_op jit(solution)/shard_map/ppermute | solution.py:258
  31.2 0.5 %collective-permute-start.1 = (f32[3,72,32]{1,2,0:T(8,128)S(1)}, f32[3,72,32]{1,2,0:T(8,128)S(1)}, u32[]{:S(2)}, u32[]{:S(2)}) collective-permute-start(f32[3,72,32]{1,2,0:T(8,128)S(1)} %bitcast.44), channel_id=1, source_target_pairs={{0,2},{1,3},{2,0},{3,1},{4,6},{5,7},{6,4},{7,5},{8,10},{9,11},{10,... | collective-permute-start | bytes 82952 | tf_op jit(solution)/shard_map/ppermute | solution.py:258
  31.7 0.6 %collective-permute-start = (f32[3,72,32]{1,2,0:T(8,128)S(1)}, f32[3,72,32]{1,2,0:T(8,128)S(1)}, u32[]{:S(2)}, u32[]{:S(2)}) collective-permute-start(f32[3,72,32]{1,2,0:T(8,128)S(1)} %bitcast.43), channel_id=1, source_target_pairs={{0,1},{1,2},{2,3},{3,0},{4,5},{5,6},{6,7},{7,4},{8,9},{9,10},{10,1... | collective-permute-start | bytes 82952 | tf_op jit(solution)/shard_map/ppermute | solution.py:258
  32.3 2.6 %collective-permute-done.2 = f32[3,72,32]{1,2,0:T(8,128)S(1)} collective-permute-done((f32[3,72,32]{1,2,0:T(8,128)S(1)}, f32[3,72,32]{1,2,0:T(8,128)S(1)}, u32[]{:S(2)}, u32[]{:S(2)}) %collective-permute-start.2) | collective-permute-done | bytes 27680 | tf_op jit(solution)/shard_map/ppermute | solution.py:258
  34.9 1.6 %collective-permute-done.1 = f32[3,72,32]{1,2,0:T(8,128)S(1)} collective-permute-done((f32[3,72,32]{1,2,0:T(8,128)S(1)}, f32[3,72,32]{1,2,0:T(8,128)S(1)}, u32[]{:S(2)}, u32[]{:S(2)}) %collective-permute-start.1) | collective-permute-done | bytes 27680 | tf_op jit(solution)/shard_map/ppermute | solution.py:258
  36.6 1.9 %collective-permute-done = f32[3,72,32]{1,2,0:T(8,128)S(1)} collective-permute-done((f32[3,72,32]{1,2,0:T(8,128)S(1)}, f32[3,72,32]{1,2,0:T(8,128)S(1)}, u32[]{:S(2)}, u32[]{:S(2)}) %collective-permute-start) | collective-permute-done | bytes 27680 | tf_op jit(solution)/shard_map/ppermute | solution.py:258
  38.5 0.6 %gather_fusion = f32[4,3,72,32]{2,3,1,0:T(8,128)S(1)} fusion(f32[4,3,72,32]{2,3,1,0:T(8,128)S(1)} %pad_maximum_fusion, s32[1024]{0:T(1024)S(1)} %pad_clamp_fusion), kind=kCustom, calls=%fused_computation | custom fusion | bytes 221200 | tf_op jit(solution)/shard_map/jit(_take)/gather | solution.py:261
  39.0 0.1 select_bitcast_fusion
  39.1 0.8 %copy.21.self_ref = f32[3,72,128]{2,1,0:T(8,128)} copy(f32[3,72,128]{1,2,0:T(8,128)S(1)} %bitcast.39) | data formatting | bytes 221184 | tf_op jit(solution)/shard_map/reshape | solution.py:261
  39.9 0.1 all-to-all-done.got_ref
  40.0 0.0 copy-start
  40.0 0.9 %copy-done = bf16[128,24,128]{2,1,0:T(8,128)(2,1)} copy-done((bf16[128,24,128]{2,1,0:T(8,128)(2,1)}, bf16[128,24,128]{2,1,0:T(8,128)(2,1)S(1)}, u32[]{:S(2)}) %copy-start) | copy-done | bytes 786456
  40.9 2.7 %solve.1 = f32[3,72,128]{2,1,0:T(8,128)} custom-call(s32[1]{0:T(128)} %bitcast.group_ref, bf16[128,24,128]{2,1,0:T(8,128)(2,1)} %copy-done, f32[3,72,128]{2,1,0:T(8,128)} %copy.21.self_ref, f32[3,3,4,128]{3,2,1,0:T(4,128)} %bitcast.49), custom_call_target="tpu_custom_call" | custom-call | tf_op jit(solution)/shard_map/solve/pallas_call | solution.py:213
  (5 shorter events, 0.1 us)
Async XLA Ops:
  11.9 28.2 %all-to-all-start = ((bf16[128,24,128]{2,1,0:T(8,128)(2,1)}), bf16[128,24,128]{2,1,0:T(8,128)(2,1)S(1)}, u32[]{:S(2)}, u32[]{:S(2)}) async-start(bf16[128,24,128]{2,1,0:T(8,128)(2,1)} %bitcast.35), calls=%async_computation | async-start | bytes 1572864 | tf_op jit(solution)/shard_map/all_to_all | solution.py:249
  28.4 6.5 %collective-permute-start.2 = (f32[3,72,32]{1,2,0:T(8,128)S(1)}, f32[3,72,32]{1,2,0:T(8,128)S(1)}, u32[]{:S(2)}, u32[]{:S(2)}) collective-permute-start(f32[3,72,32]{1,2,0:T(8,128)S(1)} %bitcast.46), channel_id=1, source_target_pairs={{0,3},{1,0},{2,1},{3,2},{4,7},{5,4},{6,5},{7,6},{8,11},{9,8},{10,9... | collective-permute-start | bytes 82952 | tf_op jit(solution)/shard_map/ppermute | solution.py:258
  31.2 5.4 %collective-permute-start.1 = (f32[3,72,32]{1,2,0:T(8,128)S(1)}, f32[3,72,32]{1,2,0:T(8,128)S(1)}, u32[]{:S(2)}, u32[]{:S(2)}) collective-permute-start(f32[3,72,32]{1,2,0:T(8,128)S(1)} %bitcast.44), channel_id=1, source_target_pairs={{0,2},{1,3},{2,0},{3,1},{4,6},{5,7},{6,4},{7,5},{8,10},{9,11},{10,... | collective-permute-start | bytes 82952 | tf_op jit(solution)/shard_map/ppermute | solution.py:258
  31.7 6.7 %collective-permute-start = (f32[3,72,32]{1,2,0:T(8,128)S(1)}, f32[3,72,32]{1,2,0:T(8,128)S(1)}, u32[]{:S(2)}, u32[]{:S(2)}) collective-permute-start(f32[3,72,32]{1,2,0:T(8,128)S(1)} %bitcast.43), channel_id=1, source_target_pairs={{0,1},{1,2},{2,3},{3,0},{4,5},{5,6},{6,7},{7,4},{8,9},{9,10},{10,1... | collective-permute-start | bytes 82952 | tf_op jit(solution)/shard_map/ppermute | solution.py:258
  40.0 0.9 %copy-start = (bf16[128,24,128]{2,1,0:T(8,128)(2,1)}, bf16[128,24,128]{2,1,0:T(8,128)(2,1)S(1)}, u32[]{:S(2)}) copy-start(bf16[128,24,128]{2,1,0:T(8,128)(2,1)S(1)} %all-to-all-done.got_ref) | copy-start | bytes 2359300

commit v2 on v1

v2 whole, which is shorter than its diff:
```python
import jax
import jax.numpy as jnp
from jax import lax
from jax.experimental import pallas as pl
from jax.experimental.pallas import tpu as pltpu
from jax.sharding import PartitionSpec as P

LANES = 128
NN = (((1,), (0,)), ((), ()))
NT = (((1,), (1,)), ((), ()))
TN = (((0,), (0,)), ((), ()))
SLOTS = 12
ROWS = 2 * SLOTS


def mm(a, b, dims=NN):
    return lax.dot_general(a, b, dims, preferred_element_type=jnp.float32)


def split(x):
    high = x.astype(jnp.bfloat16)
    return high, (x - high.astype(jnp.float32)).astype(jnp.bfloat16)


def columns(x, count):
    return jnp.concatenate(
        [jnp.broadcast_to(x[:, v : v + 1], (x.shape[0], LANES)) for v in range(count)], axis=0
    )


def route(dest, ident, ves_count):
    near, ves = dest.shape
    pairs = near * ves
    lane = lax.broadcasted_iota(jnp.int32, (pairs, LANES), 1)
    hot = jnp.where(columns(dest, ves) == lane, 1.0, 0.0)
    earlier = jnp.where(
        lax.broadcasted_iota(jnp.int32, (pairs, pairs), 0)
        > lax.broadcasted_iota(jnp.int32, (pairs, pairs), 1),
        1.0,
        0.0,
    ).astype(jnp.bfloat16)
    counts = mm(earlier, hot.astype(jnp.bfloat16))
    ones = jnp.ones((8, LANES), jnp.bfloat16)
    rank = mm(ones, (hot * counts).astype(jnp.bfloat16), NT)
    place = mm(ones, (hot * (lane + 1).astype(jnp.float32)).astype(jnp.bfloat16), NT)
    ids = jnp.where(lane == 0, columns(ident.astype(jnp.float32), ves), 0.0)
    ids = mm(ones, ids.astype(jnp.bfloat16), NT)
    slot = ((place - 1.0) * SLOTS + rank)[:1].astype(jnp.int32)
    shape = (ves_count, ROWS, pairs)
    row = lax.broadcasted_iota(jnp.int32, shape, 1)
    base = lax.broadcasted_iota(jnp.int32, shape, 0) * SLOTS
    tile, inner = row // 8, row % 8
    code = (base + jnp.where(tile == 2, 8 + inner % 4, inner)).reshape(-1, pairs)
    upper = jnp.where(tile == 2, inner // 4, tile).reshape(-1, pairs)
    match = code == slot
    pick = [jnp.where(match & (upper == half), 1.0, 0.0) for half in range(2)]
    return jnp.concatenate(pick, axis=1).astype(jnp.bfloat16), ids


def pairs_kernel(
    live_ref, adj_hbm, up_hbm, down_hbm, radial_hbm, dist_hbm, owner_hbm, local_hbm, analysis_hbm,
    out_ref,
    adj_ref, up_ref, down_ref, radial_ref, dist_ref, owner_ref, local_ref, analysis_ref,
    ups_ref, field_ref, m_ref, sem,
):
    comps, ves, points = adj_ref.shape
    fine = up_ref.shape[1]
    near = dist_ref.shape[0]
    pairs = near * ves
    ves_count, groups = out_ref.shape[:2]
    wide = analysis_ref.shape[0] // groups
    half = fine // 2 // 256 * 256

    def fetch(i, source, target):
        copy = pltpu.make_async_copy(source, target, sem.at[i])
        copy.start()
        return copy

    small = [
        fetch(0, owner_hbm, owner_ref),
        fetch(1, local_hbm, local_ref),
        fetch(2, dist_hbm, dist_ref),
        fetch(3, radial_hbm, radial_ref.at[0]),
    ]
    get_analysis = fetch(4, analysis_hbm, analysis_ref)
    get_down = fetch(5, down_hbm.at[:, :half], down_ref.at[:, :half])
    get_rest = fetch(6, down_hbm.at[:, half:], down_ref.at[:, half:])
    get_adj = fetch(7, adj_hbm, adj_ref)
    get_up = fetch(8, up_hbm, up_ref)

    for copy in small:
        copy.wait()
    owner = owner_ref[...]
    order = lax.broadcasted_iota(jnp.int32, owner.shape, 1) * near + lax.broadcasted_iota(
        jnp.int32, owner.shape, 0
    )
    dest = jnp.where(order < live_ref[0], owner // groups, -1)
    pick, ids = route(dest, (owner % groups) * ves + local_ref[...], ves_count)
    dist = columns(dist_ref[...], ves)

    get_analysis.wait()
    high, low = split(analysis_ref[...])
    even = points // 256 * 256
    tails = jnp.concatenate([high[:, even:], low[:, even:]], axis=1)

    def project(start, stop):
        at = slice(start, stop)
        body = down_ref[:even, at]
        tail = down_ref[even:, at]
        m = mm(high[:, :even], body) + mm(low[:, :even], body)
        m_ref[:, at] = (m + mm(tails, jnp.concatenate([tail, tail], axis=0))).astype(jnp.bfloat16)

    def fields(start, stop):
        for s in range(start, stop, LANES):
            size = min(LANES, stop - s)
            at = slice(s, s + size)
            weight = 1.0 / (1.0 + dist[:, :size] * radial_ref[:, at])
            for c in range(comps):
                ups = [
                    jnp.broadcast_to(ups_ref[c * ves + v : c * ves + v + 1, at], (near, size))
                    for v in range(ves)
                ]
                value = jnp.concatenate(ups, axis=0) * weight
                field_ref[c * pairs : (c + 1) * pairs, at] = value.astype(jnp.bfloat16)

    get_down.wait()
    for s in range(0, half, 256):
        project(s, s + 256)
    get_adj.wait()
    get_up.wait()
    ups_ref[...] = mm(adj_ref[...].reshape(comps * ves, points), up_ref[...])
    get_rest.wait()
    for s in range(half, fine, 256):
        project(s, min(s + 256, fine))
        fields(s - half, min(s - half + 256, half))
        fields(s, min(s + 256, fine))
    part = mm(m_ref[...], field_ref[...], NT)

    zeros = jnp.zeros((2 * LANES - 3 * wide - 8, pairs), jnp.float32)

    def message(g):
        p = [part[g * wide : (g + 1) * wide, c * pairs : (c + 1) * pairs] for c in range(comps)]
        low_half = jnp.concatenate([p[0], p[1][: LANES - wide]], axis=0)
        high_half = jnp.concatenate([p[1][LANES - wide :], p[2], zeros, ids], axis=0)
        return jnp.concatenate([low_half, high_half], axis=1).astype(jnp.bfloat16)

    for g in range(0, groups, 2):
        sent = mm(pick, jnp.concatenate([message(g), message(g + 1)], axis=0), NT)
        for i in range(2):
            block = sent[:, i * LANES : (i + 1) * LANES]
            out_ref[:, g + i] = block.reshape(ves_count, ROWS, LANES).astype(jnp.bfloat16)


def call_pairs(ves_count, groups, live, adj, up, down, radial, dist, owner, local, analysis):
    comps, ves, _ = adj.shape
    fine = up.shape[1]
    pairs = ves * dist.shape[0]
    like = lambda a: pltpu.VMEM(a.shape, a.dtype)
    return pl.pallas_call(
        pairs_kernel,
        out_shape=jax.ShapeDtypeStruct((ves_count, groups, ROWS, LANES), jnp.bfloat16),
        in_specs=[pl.BlockSpec(memory_space=pltpu.SMEM)] + [pl.BlockSpec(memory_space=pl.ANY)] * 8,
        out_specs=pl.BlockSpec(memory_space=pltpu.VMEM),
        scratch_shapes=[
            like(adj), like(up), like(down), pltpu.VMEM((1, fine), jnp.float32),
            like(dist), like(owner), like(local), like(analysis),
            pltpu.VMEM((comps * ves, fine), jnp.float32),
            pltpu.VMEM((comps * pairs, fine), jnp.bfloat16),
            pltpu.VMEM((analysis.shape[0], fine), jnp.bfloat16),
            pltpu.SemaphoreType.DMA((9,)),
        ],
        compiler_params=pltpu.CompilerParams(vmem_limit_bytes=62 * 1024 * 1024),
        name="pairs",
    )(live, adj, up, down, radial, dist, owner, local, analysis)


def self_kernel_body(group_ref, adj_ref, jac_ref, kernel_ref, analysis_ref, *refs):
    *outs, s_ref = refs
    comps, ves, points = adj_ref.shape
    groups, wide, _ = s_ref.shape
    high, low = split(analysis_ref[...])
    s = mm(high, kernel_ref[...], NT) + mm(low, kernel_ref[...], NT)
    for g in range(groups):
        s_ref[g] = s[g * wide : (g + 1) * wide]
    scaled = (adj_ref[...].astype(jnp.float32) * jac_ref[...].astype(jnp.float32)[None]).astype(
        jnp.bfloat16
    )
    scaled = scaled.reshape(comps * ves, points)
    for i, out in enumerate(outs):
        s_high, s_low = split(s_ref[(group_ref[0] + i) % groups])
        value = mm(scaled, s_high, NT) + mm(scaled, s_low, NT)
        out[...] = jnp.concatenate(
            [value, jnp.zeros((comps * ves, LANES - wide), jnp.float32)], axis=1
        )


def call_self(groups, group, adj, jac, kernel, analysis):
    comps, ves, points = adj.shape
    vmem = pl.BlockSpec(memory_space=pltpu.VMEM)
    return pl.pallas_call(
        self_kernel_body,
        out_shape=[jax.ShapeDtypeStruct((comps * ves, LANES), jnp.float32)] * groups,
        in_specs=[pl.BlockSpec(memory_space=pltpu.SMEM)] + [vmem] * 4,
        out_specs=[vmem] * groups,
        scratch_shapes=[pltpu.VMEM((groups, analysis.shape[0] // groups, points), jnp.float32)],
        compiler_params=pltpu.CompilerParams(vmem_limit_bytes=16 * 1024 * 1024),
        name="self_term",
    )(group, adj, jac, kernel, analysis)


def solve_kernel(group_ref, got_ref, blocks_ref, *refs):
    *selfs, out_ref, self_ref = refs
    senders, rows, lanes = got_ref.shape
    comps, wide, ves = out_ref.shape
    groups = len(selfs)
    ves_dev = ves // groups
    group = group_ref[0]
    for i, ref in enumerate(selfs):
        self_ref[(group + groups - i) % groups] = ref[...]
    lane = lax.broadcasted_iota(jnp.int32, (senders, 8, lanes), 2).astype(jnp.float32)
    row = lax.broadcasted_iota(jnp.int32, (senders, 8, lanes), 1)
    first = got_ref[:, 8:16, lanes - 1 : lanes].astype(jnp.float32)
    other = got_ref[:, 16:24, lanes - 1 : lanes].astype(jnp.float32)
    first = jnp.where(first == lane, 1.0, 0.0)
    other = jnp.where(other == lane, 1.0, 0.0)
    zero = jnp.zeros_like(first)
    to_low = [first, zero, jnp.where(row < 4, pltpu.roll(other, 4, 1), 0.0)]
    to_high = [zero, first, jnp.where(row < 4, 0.0, other)]
    flat = got_ref[...].reshape(senders * rows, lanes)

    def gather(to):
        to = jnp.concatenate(to, axis=1).reshape(senders * rows, lanes).astype(jnp.bfloat16)
        return mm(flat, to, TN)

    near_low = gather(to_low)
    near_high = gather(to_high)
    cut = 2 * wide - lanes
    near = [
        near_low[:wide],
        jnp.concatenate([near_low[wide:], near_high[:cut]], axis=0),
        near_high[cut : cut + wide],
    ]
    rhs = []
    for c in range(comps):
        own = [self_ref[d, c * ves_dev : (c + 1) * ves_dev] for d in range(groups)]
        own = jnp.concatenate(own, axis=0).T[:wide]
        rhs.append((own + near[c]).astype(jnp.bfloat16).astype(jnp.float32))
    at = lax.broadcasted_iota(jnp.int32, (wide, ves), 0)
    half = wide // 2

    def spread(r, c):
        b = [jnp.broadcast_to(blocks_ref[r, c, d : d + 1, :], (wide, ves)) for d in range(4)]
        lower = jnp.where(at < 4 * group + 3, b[0], b[1])
        upper = jnp.where(at < 4 * group + 5 + half, b[2], b[3])
        return jnp.where(at < half, lower, upper)

    m = [[spread(r, c) for c in range(3)] for r in range(3)]
    for c, value in enumerate(solve_three(m, rhs)):
        out_ref[c] = value


def solve_three(matrix, rhs):
    cofactor = [
        [
            matrix[1][1] * matrix[2][2] - matrix[1][2] * matrix[2][1],
            matrix[1][2] * matrix[2][0] - matrix[1][0] * matrix[2][2],
            matrix[1][0] * matrix[2][1] - matrix[1][1] * matrix[2][0],
        ],
        [
            matrix[0][2] * matrix[2][1] - matrix[0][1] * matrix[2][2],
            matrix[0][0] * matrix[2][2] - matrix[0][2] * matrix[2][0],
            matrix[0][1] * matrix[2][0] - matrix[0][0] * matrix[2][1],
        ],
        [
            matrix[0][1] * matrix[1][2] - matrix[0][2] * matrix[1][1],
            matrix[0][2] * matrix[1][0] - matrix[0][0] * matrix[1][2],
            matrix[0][0] * matrix[1][1] - matrix[0][1] * matrix[1][0],
        ],
    ]
    determinant = (
        matrix[0][0] * cofactor[0][0]
        + matrix[0][1] * cofactor[0][1]
        + matrix[0][2] * cofactor[0][2]
    )
    return [
        (cofactor[0][col] * rhs[0] + cofactor[1][col] * rhs[1] + cofactor[2][col] * rhs[2])
        / determinant
        for col in range(3)
    ]


def call_solve(wide, group, got, blocks, selfs):
    comps = blocks.shape[0]
    ves = blocks.shape[-1]
    vmem = pl.BlockSpec(memory_space=pltpu.VMEM)
    return pl.pallas_call(
        solve_kernel,
        out_shape=jax.ShapeDtypeStruct((comps, wide, ves), jnp.float32),
        in_specs=[pl.BlockSpec(memory_space=pltpu.SMEM)] + [vmem] * (2 + len(selfs)),
        out_specs=vmem,
        scratch_shapes=[pltpu.VMEM((len(selfs),) + selfs[0].shape, jnp.float32)],
        compiler_params=pltpu.CompilerParams(vmem_limit_bytes=24 * 1024 * 1024),
        name="solve",
    )(group, got, blocks, *selfs)


def body(
    adj_velocity,
    jacobian,
    self_kernel,
    near_kernel_up,
    near_kernel_down,
    radial,
    near_dist,
    near_owner,
    near_local,
    live_pairs,
    analysis,
    blocks,
):
    ves_count, groups = lax.axis_size("ves"), lax.axis_size("deg")
    group = lax.axis_index("deg").astype(jnp.int32)[None]
    adj = adj_velocity.transpose(1, 0, 2)
    projection = analysis.T
    sent = call_pairs(
        ves_count, groups, live_pairs, adj, near_kernel_up, near_kernel_down.T, radial,
        near_dist.T, near_owner.T, near_local.T, projection,
    )
    sent, late = lax.optimization_barrier((sent, group))
    got = lax.all_to_all(
        sent.reshape(ves_count * groups, ROWS, LANES),
        ("ves", "deg"),
        split_axis=0,
        concat_axis=0,
        tiled=True,
    )
    selfs = call_self(groups, late, adj, jacobian, self_kernel, projection)
    selfs = [selfs[0]] + [
        lax.ppermute(selfs[i], "deg", [(j, (j + i) % groups) for j in range(groups)])
        for i in range(1, groups)
    ]
    return call_solve(
        analysis.shape[1] // groups, group, got, blocks.transpose(1, 2, 0, 3), selfs
    )


def solution(mesh):
    return jax.shard_map(
        body,
        mesh=mesh,
        in_specs=(
            P(("ves", "deg"), None, None),
            P(("ves", "deg"), None),
            P(),
            P(),
            P(),
            P(),
            P(("ves", "deg"), None),
            P(("ves", "deg"), None),
            P(("ves", "deg"), None),
            P(("ves", "deg")),
            P(),
            P("deg", None, None, "ves"),
        ),
        out_specs=P(None, "deg", "ves"),
        check_vma=False,
    )
```

time: 43.9 us -> 38 us (0.87)
  Pallas kernels: 16.3 us -> 10.3 us
  local copies, waits for them, and re-layouts: 4.82 us -> 0.02 us
  waiting for transfers between devices: 6.24 us -> 10.2 us
  starting transfers between devices: 15.3 us -> 16.5 us
    pallas_call x3, Pallas kernels: 16.3 us -> 10.3 us  [the longest x1 7.42 us: call_pairs(): pl.pallas_call(pairs_kernel, out_shape=jax.ShapeDtypeStruct((ves_count, g...]
    all_to_all x1, waiting for transfers between devices: 0.13 us -> 2.82 us  [body(): lax.all_to_all(sent.reshape(ves_count * groups, ROWS, LANES), ('ves', 'de...]
    reshape x2 -> x0, local copies, waits for them, and re-layouts: 1.82 us -> none  [the longest x1 1.06 us: body(): own = own.reshape(comps, ves_dev, groups, wide).transpose(2, 0, 3, 1)]
    broadcast_in_dim x1 -> x0, local copies, waits for them, and re-layouts: 1.31 us -> none  [body(): radial[None, :]]
    ppermute x3, waiting for transfers between devices: 6.11 us -> 7.34 us  [body(): lax.ppermute(selfs[i], 'deg', [(j, (j + i) % groups) for j in range(group...]
    ppermute x3, starting transfers between devices: 3.83 us -> 5.02 us  [body(): lax.ppermute(selfs[i], 'deg', [(j, (j + i) % groups) for j in range(group...]
    unnamed x2 -> x10, local copies, waits for them, and re-layouts: 0.89 us -> 0.02 us
    gather x1 -> x0, local copies, waits for them, and re-layouts: 0.56 us -> none  [body(): jnp.take(stacked, order, axis=0).transpose(1, 2, 0, 3)]
  transfers between devices with their start and end apart: 4 -> 4, of which waited for: 4 -> 3; matrix products, arithmetic and copies ran while one was open for 6% -> 0% of each run, Pallas kernels for 9% -> 4%
where the time goes in v2:
time: 38 us; the launch traced here: 37.8 us
  starting transfers between devices  16.5 us (43%)
  Pallas kernels  10.3 us (27%)
  waiting for transfers between devices  10.2 us (27%)
  between operations  0.75 us (2%)
    all_to_all x1, starting transfers between devices, body(): lax.all_to_all(sent.reshape(ves_count * groups, ROWS, LANES), ('ves', 'de...  11.5 us
    pallas_call x1, Pallas kernels, call_pairs(): pl.pallas_call(pairs_kernel, out_shape=jax.ShapeDtypeStruct((ves_count, g...  7.42 us
    ppermute x3, waiting for transfers between devices, body(): lax.ppermute(selfs[i], 'deg', [(j, (j + i) % groups) for j in range(group...  7.34 us
    ppermute x3, starting transfers between devices, body(): lax.ppermute(selfs[i], 'deg', [(j, (j + i) % groups) for j in range(group...  5.02 us
    all_to_all x1, waiting for transfers between devices, body(): lax.all_to_all(sent.reshape(ves_count * groups, ROWS, LANES), ('ves', 'de...  2.82 us
    pallas_call x1, Pallas kernels, call_solve(): pl.pallas_call(solve_kernel, out_shape=jax.ShapeDtypeStruct((comps, wide,...  1.5 us
    pallas_call x1, Pallas kernels, call_self(): pl.pallas_call(self_kernel_body, out_shape=[jax.ShapeDtypeStruct((comps *...  1.42 us
  transfers between devices with their start and end apart: 4, of which 3 were waited for; matrix products, arithmetic and copies ran while one was open for 0% of the time, Pallas kernels for 4%

profile of v2, /device:TPU:1, one launch (start us, length us, event | category | flops | bytes accessed | tf_op | source)
XLA Modules:
  0.0 37.8 jit_solution(16381889589671354756)
XLA Ops:
  0.7 0.0 copy-start
  0.7 0.0 copy-start.1
  0.7 0.0 copy-start.2
  0.7 0.0 copy-start.3
  0.7 7.4 %pairs.1 = bf16[32,4,24,128]{3,2,1,0:T(8,128)(2,1)} custom-call(s32[1]{0:T(128)S(6)} %copy.13.live_ref, bf16[3,32,544]{2,1,0:T(8,128)(2,1)} %bitcast.11, bf16[544,2112]{1,0:T(8,128)(2,1)} %up_hbm.1, bf16[544,2112]{1,0:T(8,128)(2,1)} %bitcast.15, f32[2112]{0:T(1024)} %radial_hbm.1, f32[8,32]{1,0:T(8,128)} %bitcast.16, s32[8,32]{1,0:T(8,128)} %bitcast.17, ...), custom_call_target="tpu_custom_call" | custom-call | tf_op jit(solution)/shard_map/pairs/pallas_call | solution.py:159
  8.1 0.0 copy-start.4
  8.1 11.5 %all-to-all-start = ((bf16[128,24,128]{2,1,0:T(8,128)(2,1)}), bf16[128,24,128]{2,1,0:T(8,128)(2,1)S(1)}, u32[]{:S(2)}, u32[]{:S(2)}) async-start(bf16[128,24,128]{2,1,0:T(8,128)(2,1)} %bitcast.14), calls=%async_computation | async-start | bytes 1572864 | tf_op jit(solution)/shard_map/all_to_all | solution.py:330
  19.7 0.0 copy-done
  19.7 0.0 copy-done.1
  19.7 0.0 copy-done.2
  19.7 0.0 copy-done.3
  19.7 1.4 %self_term.1 = (f32[96,128]{1,0:T(8,128)S(1)}, f32[96,128]{1,0:T(8,128)S(1)}, f32[96,128]{1,0:T(8,128)S(1)}, f32[96,128]{1,0:T(8,128)S(1)}) custom-call(s32[1]{0:T(128)} %bitcast.group_ref, bf16[3,32,544]{2,1,0:T(8,128)(2,1)S(1)} %bitcast.12, bf16[32,544]{1,0:T(8,128)(2,1)S(1)} %copy-done.3, bf16[544,544]{1,0:T(8,128)(2,1)S(1)} %copy-done.1, ...), custom_call_target="tpu_custom_call" | custom-call | tf_op jit(solution)/shard_map/self_term/pallas_call | solution.py:200
  21.1 1.4 %collective-permute-start = (f32[96,128]{1,0:T(8,128)S(1)}, f32[96,128]{1,0:T(8,128)S(1)}, u32[]{:S(2)}, u32[]{:S(2)}) collective-permute-start(f32[96,128]{1,0:T(8,128)S(1)} %get-tuple-element.14), channel_id=1, source_target_pairs={{0,1},{1,2},{2,3},{3,0},{4,5},{5,6},{6,7},{7,4},{8,9},{9,10},{10,1... | collective-permute-start | bytes 147464 | tf_op jit(solution)/shard_map/ppermute | solution.py:339
  22.6 2.4 %collective-permute-start.1 = (f32[96,128]{1,0:T(8,128)S(1)}, f32[96,128]{1,0:T(8,128)S(1)}, u32[]{:S(2)}, u32[]{:S(2)}) collective-permute-start(f32[96,128]{1,0:T(8,128)S(1)} %get-tuple-element.15), channel_id=1, source_target_pairs={{0,2},{1,3},{2,0},{3,1},{4,6},{5,7},{6,4},{7,5},{8,10},{9,11},{10,... | collective-permute-start | bytes 147464 | tf_op jit(solution)/shard_map/ppermute | solution.py:339
  25.0 1.1 %collective-permute-start.2 = (f32[96,128]{1,0:T(8,128)S(1)}, f32[96,128]{1,0:T(8,128)S(1)}, u32[]{:S(2)}, u32[]{:S(2)}) collective-permute-start(f32[96,128]{1,0:T(8,128)S(1)} %get-tuple-element.16), channel_id=1, source_target_pairs={{0,3},{1,0},{2,1},{3,2},{4,7},{5,4},{6,5},{7,6},{8,11},{9,8},{10,9... | collective-permute-start | bytes 147464 | tf_op jit(solution)/shard_map/ppermute | solution.py:339
  26.1 3.4 %collective-permute-done.refs_1_ = f32[96,128]{1,0:T(8,128)S(1)} collective-permute-done((f32[96,128]{1,0:T(8,128)S(1)}, f32[96,128]{1,0:T(8,128)S(1)}, u32[]{:S(2)}, u32[]{:S(2)}) %collective-permute-start) | collective-permute-done | bytes 49184 | tf_op jit(solution)/shard_map/ppermute | solution.py:339
  29.5 3.9 %collective-permute-done.1.refs_2_ = f32[96,128]{1,0:T(8,128)S(1)} collective-permute-done((f32[96,128]{1,0:T(8,128)S(1)}, f32[96,128]{1,0:T(8,128)S(1)}, u32[]{:S(2)}, u32[]{:S(2)}) %collective-permute-start.1) | collective-permute-done | bytes 49184 | tf_op jit(solution)/shard_map/ppermute | solution.py:339
  33.5 0.0 collective-permute-done.2.refs_3_
  33.5 2.8 %all-to-all-done.got_ref = bf16[128,24,128]{2,1,0:T(8,128)(2,1)S(1)} async-done(((bf16[128,24,128]{2,1,0:T(8,128)(2,1)}), bf16[128,24,128]{2,1,0:T(8,128)(2,1)S(1)}, u32[]{:S(2)}, u32[]{:S(2)}) %all-to-all-start) | async-done | bytes 786464 | tf_op jit(solution)/shard_map/all_to_all | solution.py:330
  36.3 0.0 copy-done.4
  36.3 1.5 %solve.1 = f32[3,72,128]{2,1,0:T(8,128)} custom-call(s32[1]{0:T(128)} %bitcast.group_ref, bf16[128,24,128]{2,1,0:T(8,128)(2,1)S(1)} %all-to-all-done.got_ref, f32[3,3,4,128]{3,2,1,0:T(4,128)S(1)} %bitcast.13, f32[96,128]{1,0:T(8,128)S(1)} %get-tuple-element.13.refs_0_, f32[96,128]{1,0:T(8,128)S(1)} %collective-permute-done.refs_1_, ...), custom_call_target="tpu_custom_call" | custom-call | tf_op jit(solution)/shard_map/solve/pallas_call | solution.py:296
Async XLA Ops:
  0.7 19.0 %copy-start = (f32[544,288]{0,1:T(8,128)S(1)}, f32[544,288]{0,1:T(8,128)}, u32[]{:S(2)}) copy-start(f32[544,288]{0,1:T(8,128)} %param.22) | copy-start | bytes 1880068
  0.7 19.0 %copy-start.1 = (bf16[544,544]{1,0:T(8,128)(2,1)S(1)}, bf16[544,544]{1,0:T(8,128)(2,1)}, u32[]{:S(2)}) copy-start(bf16[544,544]{1,0:T(8,128)(2,1)} %kernel_ref.1) | copy-start | bytes 1775620
  0.7 19.0 %copy-start.2 = (bf16[32,3,544]{2,0,1:T(8,128)(2,1)S(1)}, bf16[32,3,544]{2,0,1:T(8,128)(2,1)}, u32[]{:S(2)}) copy-start(bf16[32,3,544]{2,0,1:T(8,128)(2,1)} %param.12) | copy-start | bytes 313348
  0.7 19.0 %copy-start.3 = (bf16[32,544]{1,0:T(8,128)(2,1)S(1)}, bf16[32,544]{1,0:T(8,128)(2,1)}, u32[]{:S(2)}) copy-start(bf16[32,544]{1,0:T(8,128)(2,1)} %jac_ref.1) | copy-start | bytes 104452
  8.1 28.2 %copy-start.4 = (f32[4,3,3,128]{3,0,2,1:T(4,128)S(1)}, f32[4,3,3,128]{3,0,2,1:T(4,128)}, u32[]{:S(2)}) copy-start(f32[4,3,3,128]{3,0,2,1:T(4,128)} %param.23) | copy-start | bytes 55300
  8.1 28.2 %all-to-all-start = ((bf16[128,24,128]{2,1,0:T(8,128)(2,1)}), bf16[128,24,128]{2,1,0:T(8,128)(2,1)S(1)}, u32[]{:S(2)}, u32[]{:S(2)}) async-start(bf16[128,24,128]{2,1,0:T(8,128)(2,1)} %bitcast.14), calls=%async_computation | async-start | bytes 1572864 | tf_op jit(solution)/shard_map/all_to_all | solution.py:330
  21.1 8.4 %collective-permute-start = (f32[96,128]{1,0:T(8,128)S(1)}, f32[96,128]{1,0:T(8,128)S(1)}, u32[]{:S(2)}, u32[]{:S(2)}) collective-permute-start(f32[96,128]{1,0:T(8,128)S(1)} %get-tuple-element.14), channel_id=1, source_target_pairs={{0,1},{1,2},{2,3},{3,0},{4,5},{5,6},{6,7},{7,4},{8,9},{9,10},{10,1... | collective-permute-start | bytes 147464 | tf_op jit(solution)/shard_map/ppermute | solution.py:339
  22.6 10.9 %collective-permute-start.1 = (f32[96,128]{1,0:T(8,128)S(1)}, f32[96,128]{1,0:T(8,128)S(1)}, u32[]{:S(2)}, u32[]{:S(2)}) collective-permute-start(f32[96,128]{1,0:T(8,128)S(1)} %get-tuple-element.15), channel_id=1, source_target_pairs={{0,2},{1,3},{2,0},{3,1},{4,6},{5,7},{6,4},{7,5},{8,10},{9,11},{10,... | collective-permute-start | bytes 147464 | tf_op jit(solution)/shard_map/ppermute | solution.py:339
  25.0 8.5 %collective-permute-start.2 = (f32[96,128]{1,0:T(8,128)S(1)}, f32[96,128]{1,0:T(8,128)S(1)}, u32[]{:S(2)}, u32[]{:S(2)}) collective-permute-start(f32[96,128]{1,0:T(8,128)S(1)} %get-tuple-element.16), channel_id=1, source_target_pairs={{0,3},{1,0},{2,1},{3,2},{4,7},{5,4},{6,5},{7,6},{8,11},{9,8},{10,9... | collective-permute-start | bytes 147464 | tf_op jit(solution)/shard_map/ppermute | solution.py:339

commit v3 on v2

--- a/solution.py
+++ b/solution.py
@@ -58,16 +58,17 @@
 
 
 def pairs_kernel(
-    live_ref, adj_hbm, up_hbm, down_hbm, radial_hbm, dist_hbm, owner_hbm, local_hbm, analysis_hbm,
-    out_ref,
-    adj_ref, up_ref, down_ref, radial_ref, dist_ref, owner_ref, local_ref, analysis_ref,
-    ups_ref, field_ref, m_ref, sem,
+    live_hbm, adj_hbm, up_hbm, down_hbm, radial_hbm, dist_hbm, owner_hbm, local_hbm, analysis_hbm,
+    out_hbm,
+    live_ref, adj_ref, up_ref, down_ref, radial_ref, dist_ref, owner_ref, local_ref, analysis_ref,
+    ups_ref, field_ref, m_ref, out_ref, sem,
 ):
     comps, ves, points = adj_ref.shape
     fine = up_ref.shape[1]
     near = dist_ref.shape[0]
     pairs = near * ves
-    ves_count, groups = out_ref.shape[:2]
+    groups = out_ref.shape[0]
+    ves_count = out_ref.shape[1] // ROWS
     wide = analysis_ref.shape[0] // groups
     half = fine // 2 // 256 * 256
 
@@ -81,15 +82,17 @@
         fetch(1, local_hbm, local_ref),
         fetch(2, dist_hbm, dist_ref),
         fetch(3, radial_hbm, radial_ref.at[0]),
+        fetch(10, live_hbm, live_ref),
     ]
-    get_analysis = fetch(4, analysis_hbm, analysis_ref)
-    get_down = fetch(5, down_hbm.at[:, :half], down_ref.at[:, :half])
-    get_rest = fetch(6, down_hbm.at[:, half:], down_ref.at[:, half:])
-    get_adj = fetch(7, adj_hbm, adj_ref)
-    get_up = fetch(8, up_hbm, up_ref)
-
+    get_adj = fetch(4, adj_hbm, adj_ref)
+    get_up = [fetch(5, up_hbm.at[:, :half], up_ref.at[:, :half])]
+    get_analysis = fetch(6, analysis_hbm, analysis_ref)
+    get_down = [fetch(7, down_hbm.at[:, :half], down_ref.at[:, :half])]
     for copy in small:
         copy.wait()
+    get_up.append(fetch(8, up_hbm.at[:, half:], up_ref.at[:, half:]))
+    get_down.append(fetch(9, down_hbm.at[:, half:], down_ref.at[:, half:]))
+
     owner = owner_ref[...]
     order = lax.broadcasted_iota(jnp.int32, owner.shape, 1) * near + lax.broadcasted_iota(
         jnp.int32, owner.shape, 0
@@ -97,11 +100,9 @@
     dest = jnp.where(order < live_ref[0], owner // groups, -1)
     pick, ids = route(dest, (owner % groups) * ves + local_ref[...], ves_count)
     dist = columns(dist_ref[...], ves)
-
-    get_analysis.wait()
-    high, low = split(analysis_ref[...])
+    get_adj.wait()
+    adj = adj_ref[...].reshape(comps * ves, points)
     even = points // 256 * 256
-    tails = jnp.concatenate([high[:, even:], low[:, even:]], axis=1)
 
     def project(start, stop):
         at = slice(start, stop)
@@ -123,17 +124,17 @@
                 value = jnp.concatenate(ups, axis=0) * weight
                 field_ref[c * pairs : (c + 1) * pairs, at] = value.astype(jnp.bfloat16)
 
-    get_down.wait()
-    for s in range(0, half, 256):
-        project(s, s + 256)
-    get_adj.wait()
-    get_up.wait()
-    ups_ref[...] = mm(adj_ref[...].reshape(comps * ves, points), up_ref[...])
-    get_rest.wait()
-    for s in range(half, fine, 256):
-        project(s, min(s + 256, fine))
-        fields(s - half, min(s - half + 256, half))
-        fields(s, min(s + 256, fine))
+    for i, (start, stop) in enumerate([(0, half), (half, fine)]):
+        get_up[i].wait()
+        ups_ref[:, start:stop] = mm(adj, up_ref[:, start:stop])
+        if i == 0:
+            get_analysis.wait()
+            high, low = split(analysis_ref[...])
+            tails = jnp.concatenate([high[:, even:], low[:, even:]], axis=1)
+        get_down[i].wait()
+        for s in range(start, stop, 256):
+            project(s, min(s + 256, stop))
+            fields(s, min(s + 256, stop))
     part = mm(m_ref[...], field_ref[...], NT)
 
     zeros = jnp.zeros((2 * LANES - 3 * wide - 8, pairs), jnp.float32)
@@ -144,32 +145,37 @@
         high_half = jnp.concatenate([p[1][LANES - wide :], p[2], zeros, ids], axis=0)
         return jnp.concatenate([low_half, high_half], axis=1).astype(jnp.bfloat16)
 
+    copies = []
     for g in range(0, groups, 2):
         sent = mm(pick, jnp.concatenate([message(g), message(g + 1)], axis=0), NT)
         for i in range(2):
-            block = sent[:, i * LANES : (i + 1) * LANES]
-            out_ref[:, g + i] = block.reshape(ves_count, ROWS, LANES).astype(jnp.bfloat16)
+            out_ref[g + i] = sent[:, i * LANES : (i + 1) * LANES].astype(jnp.bfloat16)
+        copies.append(fetch(11 + g // 2, out_ref.at[g : g + 2], out_hbm.at[g : g + 2]))
+    for copy in copies:
+        copy.wait()
 
 
 def call_pairs(ves_count, groups, live, adj, up, down, radial, dist, owner, local, analysis):
     comps, ves, _ = adj.shape
     fine = up.shape[1]
     pairs = ves * dist.shape[0]
+    out = (groups, ves_count * ROWS, LANES)
     like = lambda a: pltpu.VMEM(a.shape, a.dtype)
     return pl.pallas_call(
         pairs_kernel,
-        out_shape=jax.ShapeDtypeStruct((ves_count, groups, ROWS, LANES), jnp.bfloat16),
-        in_specs=[pl.BlockSpec(memory_space=pltpu.SMEM)] + [pl.BlockSpec(memory_space=pl.ANY)] * 8,
-        out_specs=pl.BlockSpec(memory_space=pltpu.VMEM),
+        out_shape=jax.ShapeDtypeStruct(out, jnp.bfloat16),
+        in_specs=[pl.BlockSpec(memory_space=pl.ANY)] * 9,
+        out_specs=pl.BlockSpec(memory_space=pl.ANY),
         scratch_shapes=[
-            like(adj), like(up), like(down), pltpu.VMEM((1, fine), jnp.float32),
+            pltpu.SMEM(live.shape, live.dtype), like(adj), like(up), like(down), pltpu.VMEM((1, fine), jnp.float32),
             like(dist), like(owner), like(local), like(analysis),
             pltpu.VMEM((comps * ves, fine), jnp.float32),
             pltpu.VMEM((comps * pairs, fine), jnp.bfloat16),
             pltpu.VMEM((analysis.shape[0], fine), jnp.bfloat16),
-            pltpu.SemaphoreType.DMA((9,)),
+            pltpu.VMEM(out, jnp.bfloat16),
+            pltpu.SemaphoreType.DMA((13,)),
         ],
-        compiler_params=pltpu.CompilerParams(vmem_limit_bytes=62 * 1024 * 1024),
+        compiler_params=pltpu.CompilerParams(vmem_limit_bytes=61 * 1024 * 1024),
         name="pairs",
     )(live, adj, up, down, radial, dist, owner, local, analysis)
 
@@ -208,15 +214,61 @@
     )(group, adj, jac, kernel, analysis)
 
 
-def solve_kernel(group_ref, got_ref, blocks_ref, *refs):
-    *selfs, out_ref, self_ref = refs
-    senders, rows, lanes = got_ref.shape
-    comps, wide, ves = out_ref.shape
+def prepare_kernel(group_ref, blocks_ref, *refs):
+    *selfs, self_ref, cofactor_ref, det_ref, order_ref = refs
     groups = len(selfs)
+    comps, wide, ves = self_ref.shape
     ves_dev = ves // groups
     group = group_ref[0]
     for i, ref in enumerate(selfs):
-        self_ref[(group + groups - i) % groups] = ref[...]
+        order_ref[(group + groups - i) % groups] = ref[...]
+    for c in range(comps):
+        own = [order_ref[d, c * ves_dev : (c + 1) * ves_dev] for d in range(groups)]
+        self_ref[c] = jnp.concatenate(own, axis=0).T[:wide]
+    at = lax.broadcasted_iota(jnp.int32, (wide, ves), 0)
+    half = wide // 2
+
+    def spread(r, c):
+        b = [jnp.broadcast_to(blocks_ref[r, c, d : d + 1, :], (wide, ves)) for d in range(4)]
+        lower = jnp.where(at < 4 * group + 3, b[0], b[1])
+        upper = jnp.where(at < 4 * group + 5 + half, b[2], b[3])
+        return jnp.where(at < half, lower, upper)
+
+    m = [[spread(r, c) for c in range(3)] for r in range(3)]
+
+    def cofactor(r, c):
+        r1, r2, c1, c2 = (r + 1) % 3, (r + 2) % 3, (c + 1) % 3, (c + 2) % 3
+        return m[r1][c1] * m[r2][c2] - m[r1][c2] * m[r2][c1]
+
+    first = [cofactor(0, c) for c in range(3)]
+    det_ref[...] = m[0][0] * first[0] + m[0][1] * first[1] + m[0][2] * first[2]
+    for r in range(3):
+        for c in range(3):
+            cofactor_ref[r, c] = first[c] if r == 0 else cofactor(r, c)
+
+
+def call_prepare(wide, group, blocks, selfs):
+    comps, ves = blocks.shape[0], blocks.shape[-1]
+    vmem = pl.BlockSpec(memory_space=pltpu.VMEM)
+    f32 = jnp.float32
+    return pl.pallas_call(
+        prepare_kernel,
+        out_shape=[
+            pltpu.VMEM((comps, wide, ves), f32),
+            pltpu.VMEM((3, 3, wide, ves), f32),
+            pltpu.VMEM((wide, ves), f32),
+        ],
+        in_specs=[pl.BlockSpec(memory_space=pltpu.SMEM)] + [vmem] * (1 + len(selfs)),
+        out_specs=[vmem] * 3,
+        scratch_shapes=[pltpu.VMEM((len(selfs),) + selfs[0].shape, f32)],
+        compiler_params=pltpu.CompilerParams(vmem_limit_bytes=16 * 1024 * 1024),
+        name="prepare",
+    )(group, blocks, *selfs)
+
+
+def solve_kernel(got_ref, self_ref, cofactor_ref, det_ref, out_ref):
+    senders, rows, lanes = got_ref.shape
+    comps, wide, ves = out_ref.shape
     lane = lax.broadcasted_iota(jnp.int32, (senders, 8, lanes), 2).astype(jnp.float32)
     row = lax.broadcasted_iota(jnp.int32, (senders, 8, lanes), 1)
     first = got_ref[:, 8:16, lanes - 1 : lanes].astype(jnp.float32)
@@ -228,80 +280,33 @@
     to_high = [zero, first, jnp.where(row < 4, 0.0, other)]
     flat = got_ref[...].reshape(senders * rows, lanes)
 
-    def gather(to):
-        to = jnp.concatenate(to, axis=1).reshape(senders * rows, lanes).astype(jnp.bfloat16)
-        return mm(flat, to, TN)
-
-    near_low = gather(to_low)
-    near_high = gather(to_high)
+    to = [jnp.concatenate(t, axis=1).reshape(senders * rows, lanes) for t in (to_low, to_high)]
+    both = mm(flat, jnp.concatenate(to, axis=1).astype(jnp.bfloat16), TN)
+    near_low, near_high = both[:, :lanes], both[:, lanes:]
     cut = 2 * wide - lanes
     near = [
         near_low[:wide],
         jnp.concatenate([near_low[wide:], near_high[:cut]], axis=0),
         near_high[cut : cut + wide],
     ]
-    rhs = []
+    rhs = [(self_ref[c] + near[c]).astype(jnp.bfloat16).astype(jnp.float32) for c in range(comps)]
+    det = det_ref[...]
     for c in range(comps):
-        own = [self_ref[d, c * ves_dev : (c + 1) * ves_dev] for d in range(groups)]
-        own = jnp.concatenate(own, axis=0).T[:wide]
-        rhs.append((own + near[c]).astype(jnp.bfloat16).astype(jnp.float32))
-    at = lax.broadcasted_iota(jnp.int32, (wide, ves), 0)
-    half = wide // 2
-
-    def spread(r, c):
-        b = [jnp.broadcast_to(blocks_ref[r, c, d : d + 1, :], (wide, ves)) for d in range(4)]
-        lower = jnp.where(at < 4 * group + 3, b[0], b[1])
-        upper = jnp.where(at < 4 * group + 5 + half, b[2], b[3])
-        return jnp.where(at < half, lower, upper)
-
-    m = [[spread(r, c) for c in range(3)] for r in range(3)]
-    for c, value in enumerate(solve_three(m, rhs)):
-        out_ref[c] = value
-
-
-def solve_three(matrix, rhs):
-    cofactor = [
-        [
-            matrix[1][1] * matrix[2][2] - matrix[1][2] * matrix[2][1],
-            matrix[1][2] * matrix[2][0] - matrix[1][0] * matrix[2][2],
-            matrix[1][0] * matrix[2][1] - matrix[1][1] * matrix[2][0],
-        ],
-        [
-            matrix[0][2] * matrix[2][1] - matrix[0][1] * matrix[2][2],
-            matrix[0][0] * matrix[2][2] - matrix[0][2] * matrix[2][0],
-            matrix[0][1] * matrix[2][0] - matrix[0][0] * matrix[2][1],
-        ],
-        [
-            matrix[0][1] * matrix[1][2] - matrix[0][2] * matrix[1][1],
-            matrix[0][2] * matrix[1][0] - matrix[0][0] * matrix[1][2],
-            matrix[0][0] * matrix[1][1] - matrix[0][1] * matrix[1][0],
-        ],
-    ]
-    determinant = (
-        matrix[0][0] * cofactor[0][0]
-        + matrix[0][1] * cofactor[0][1]
-        + matrix[0][2] * cofactor[0][2]
-    )
-    return [
-        (cofactor[0][col] * rhs[0] + cofactor[1][col] * rhs[1] + cofactor[2][col] * rhs[2])
-        / determinant
-        for col in range(3)
-    ]
-
-
-def call_solve(wide, group, got, blocks, selfs):
-    comps = blocks.shape[0]
-    ves = blocks.shape[-1]
+        out_ref[c] = (
+            cofactor_ref[0, c] * rhs[0] + cofactor_ref[1, c] * rhs[1] + cofactor_ref[2, c] * rhs[2]
+        ) / det
+
+
+def call_solve(got, prepared):
     vmem = pl.BlockSpec(memory_space=pltpu.VMEM)
     return pl.pallas_call(
         solve_kernel,
-        out_shape=jax.ShapeDtypeStruct((comps, wide, ves), jnp.float32),
-        in_specs=[pl.BlockSpec(memory_space=pltpu.SMEM)] + [vmem] * (2 + len(selfs)),
+        out_shape=jax.ShapeDtypeStruct(prepared[0].shape, jnp.float32),
+        in_specs=[vmem] * (1 + len(prepared)),
         out_specs=vmem,
-        scratch_shapes=[pltpu.VMEM((len(selfs),) + selfs[0].shape, jnp.float32)],
         compiler_params=pltpu.CompilerParams(vmem_limit_bytes=24 * 1024 * 1024),
         name="solve",
-    )(group, got, blocks, *selfs)
+    )(got, *prepared)
 
 
 def body(
@@ -328,8 +333,8 @@
     )
     sent, late = lax.optimization_barrier((sent, group))
     got = lax.all_to_all(
-        sent.reshape(ves_count * groups, ROWS, LANES),
-        ("ves", "deg"),
+        sent.reshape(groups * ves_count, ROWS, LANES),
+        ("deg", "ves"),
         split_axis=0,
         concat_axis=0,
         tiled=True,
@@ -339,9 +344,9 @@
         lax.ppermute(selfs[i], "deg", [(j, (j + i) % groups) for j in range(groups)])
         for i in range(1, groups)
     ]
-    return call_solve(
-        analysis.shape[1] // groups, group, got, blocks.transpose(1, 2, 0, 3), selfs
-    )
+    wide = analysis.shape[1] // groups
+    prepared = call_prepare(wide, group, blocks.transpose(1, 2, 0, 3), selfs)
+    return call_solve(got, prepared)
 
 
 def solution(mesh):

time: 38 us -> 37.6 us (0.989)
    ppermute x3, waiting for transfers between devices: 7.34 us -> 6.82 us  [body(): lax.ppermute(selfs[i], 'deg', [(j, (j + i) % groups) for j in range(group...]
    pallas_call x2 -> x3, Pallas kernels: 8.92 us -> 8.78 us  [the longest x1 7.35 us: call_pairs(): pl.pallas_call(pairs_kernel, out_shape=jax.ShapeDtypeStruct(out, jnp.bflo...]
where the time goes in v3:
time: 37.6 us; the launch traced here: 37.4 us
  starting transfers between devices  16.6 us (44%)
  Pallas kernels  10.2 us (27%)
  waiting for transfers between devices  9.87 us (26%)
  between operations  0.75 us (2%)
    all_to_all x1, starting transfers between devices, body(): lax.all_to_all(sent.reshape(groups * ves_count, ROWS, LANES), ('deg', 've...  11.5 us
    pallas_call x1, Pallas kernels, call_pairs(): pl.pallas_call(pairs_kernel, out_shape=jax.ShapeDtypeStruct(out, jnp.bflo...  7.35 us
    ppermute x3, waiting for transfers between devices, body(): lax.ppermute(selfs[i], 'deg', [(j, (j + i) % groups) for j in range(group...  6.82 us
    ppermute x3, starting transfers between devices, body(): lax.ppermute(selfs[i], 'deg', [(j, (j + i) % groups) for j in range(group...  5.05 us
    all_to_all x1, waiting for transfers between devices, body(): lax.all_to_all(sent.reshape(groups * ves_count, ROWS, LANES), ('deg', 've...  3.05 us
    pallas_call x1, Pallas kernels, call_self(): pl.pallas_call(self_kernel_body, out_shape=[jax.ShapeDtypeStruct((comps *...  1.41 us
    pallas_call x1, Pallas kernels, call_solve(): pl.pallas_call(solve_kernel, out_shape=jax.ShapeDtypeStruct(prepared[0].s...  1.27 us
  transfers between devices with their start and end apart: 4, of which 3 were waited for; matrix products, arithmetic and copies ran while one was open for 0% of the time, Pallas kernels for 4%

profile of v3, /device:TPU:1, one launch (start us, length us, event | category | flops | bytes accessed | tf_op | source)
XLA Modules:
  0.0 37.4 jit_solution(4272019553804263591)
XLA Ops:
  0.7 0.0 copy-start
  0.7 0.0 copy-start.1
  0.7 0.0 copy-start.2
  0.7 0.0 copy-start.3
  0.7 7.4 %pairs.1 = bf16[4,768,128]{2,1,0:T(8,128)(2,1)} custom-call(s32[1]{0:T(128)S(6)} %copy.13.live_hbm, bf16[3,32,544]{2,1,0:T(8,128)(2,1)} %bitcast.11, bf16[544,2112]{1,0:T(8,128)(2,1)} %up_hbm.1, bf16[544,2112]{1,0:T(8,128)(2,1)} %bitcast.15, f32[2112]{0:T(1024)} %radial_hbm.1, f32[8,32]{1,0:T(8,128)} %bitcast.16, s32[8,32]{1,0:T(8,128)} %bitcast.17, ...), custom_call_target="tpu_custom_call" | custom-call | tf_op jit(solution)/shard_map/pairs/pallas_call | solution.py:164
  8.1 0.0 copy-start.4
  8.1 11.5 %all-to-all-start = ((bf16[128,24,128]{2,1,0:T(8,128)(2,1)}), bf16[128,24,128]{2,1,0:T(8,128)(2,1)S(1)}, u32[]{:S(2)}, u32[]{:S(2)}) async-start(bf16[128,24,128]{2,1,0:T(8,128)(2,1)} %bitcast.14), calls=%async_computation | async-start | bytes 1572864 | tf_op jit(solution)/shard_map/all_to_all | solution.py:335
  19.6 0.0 copy-done
  19.6 0.0 copy-done.1
  19.6 0.0 copy-done.2
  19.6 0.0 copy-done.3
  19.6 1.4 %self_term.1 = (f32[96,128]{1,0:T(8,128)S(1)}, f32[96,128]{1,0:T(8,128)S(1)}, f32[96,128]{1,0:T(8,128)S(1)}, f32[96,128]{1,0:T(8,128)S(1)}) custom-call(s32[1]{0:T(128)} %bitcast.6.group_ref, bf16[3,32,544]{2,1,0:T(8,128)(2,1)S(1)} %bitcast.12, bf16[32,544]{1,0:T(8,128)(2,1)S(1)} %copy-done.3, bf16[544,544]{1,0:T(8,128)(2,1)S(1)} %copy-done.1, ...), custom_call_target="tpu_custom_call" | custom-call | tf_op jit(solution)/shard_map/self_term/pallas_call | solution.py:206
  21.0 1.5 %collective-permute-start = (f32[96,128]{1,0:T(8,128)S(1)}, f32[96,128]{1,0:T(8,128)S(1)}, u32[]{:S(2)}, u32[]{:S(2)}) collective-permute-start(f32[96,128]{1,0:T(8,128)S(1)} %get-tuple-element.17), channel_id=1, source_target_pairs={{0,1},{1,2},{2,3},{3,0},{4,5},{5,6},{6,7},{7,4},{8,9},{9,10},{10,1... | collective-permute-start | bytes 147464 | tf_op jit(solution)/shard_map/ppermute | solution.py:344
  22.5 2.5 %collective-permute-start.1 = (f32[96,128]{1,0:T(8,128)S(1)}, f32[96,128]{1,0:T(8,128)S(1)}, u32[]{:S(2)}, u32[]{:S(2)}) collective-permute-start(f32[96,128]{1,0:T(8,128)S(1)} %get-tuple-element.18), channel_id=1, source_target_pairs={{0,2},{1,3},{2,0},{3,1},{4,6},{5,7},{6,4},{7,5},{8,10},{9,11},{10,... | collective-permute-start | bytes 147464 | tf_op jit(solution)/shard_map/ppermute | solution.py:344
  24.9 1.1 %collective-permute-start.2 = (f32[96,128]{1,0:T(8,128)S(1)}, f32[96,128]{1,0:T(8,128)S(1)}, u32[]{:S(2)}, u32[]{:S(2)}) collective-permute-start(f32[96,128]{1,0:T(8,128)S(1)} %get-tuple-element.19), channel_id=1, source_target_pairs={{0,3},{1,0},{2,1},{3,2},{4,7},{5,4},{6,5},{7,6},{8,11},{9,8},{10,9... | collective-permute-start | bytes 147464 | tf_op jit(solution)/shard_map/ppermute | solution.py:344
  26.1 3.3 %collective-permute-done.refs_1_ = f32[96,128]{1,0:T(8,128)S(1)} collective-permute-done((f32[96,128]{1,0:T(8,128)S(1)}, f32[96,128]{1,0:T(8,128)S(1)}, u32[]{:S(2)}, u32[]{:S(2)}) %collective-permute-start) | collective-permute-done | bytes 49184 | tf_op jit(solution)/shard_map/ppermute | solution.py:344
  29.4 3.5 %collective-permute-done.1.refs_2_ = f32[96,128]{1,0:T(8,128)S(1)} collective-permute-done((f32[96,128]{1,0:T(8,128)S(1)}, f32[96,128]{1,0:T(8,128)S(1)}, u32[]{:S(2)}, u32[]{:S(2)}) %collective-permute-start.1) | collective-permute-done | bytes 49184 | tf_op jit(solution)/shard_map/ppermute | solution.py:344
  32.9 0.0 collective-permute-done.2.refs_3_
  32.9 0.0 copy-done.4
  32.9 0.2 prepare.1
  33.1 3.0 %all-to-all-done.got_ref = bf16[128,24,128]{2,1,0:T(8,128)(2,1)S(1)} async-done(((bf16[128,24,128]{2,1,0:T(8,128)(2,1)}), bf16[128,24,128]{2,1,0:T(8,128)(2,1)S(1)}, u32[]{:S(2)}, u32[]{:S(2)}) %all-to-all-start) | async-done | bytes 786464 | tf_op jit(solution)/shard_map/all_to_all | solution.py:335
  36.1 1.3 %solve.1 = f32[3,72,128]{2,1,0:T(8,128)} custom-call(bf16[128,24,128]{2,1,0:T(8,128)(2,1)S(1)} %all-to-all-done.got_ref, f32[3,72,128]{2,1,0:T(8,128)S(1)} %get-tuple-element.20.self_ref, f32[3,3,72,128]{3,2,1,0:T(8,128)S(1)} %get-tuple-element.21.cofactor_ref, f32[72,128]{1,0:T(8,128)S(1)} %get-tuple-element.22.det_ref), custom_call_target="tpu_custom_call" | custom-call | tf_op jit(solution)/shard_map/solve/pallas_call | solution.py:302
Async XLA Ops:
  0.7 18.9 %copy-start = (f32[544,288]{0,1:T(8,128)S(1)}, f32[544,288]{0,1:T(8,128)}, u32[]{:S(2)}) copy-start(f32[544,288]{0,1:T(8,128)} %param.22) | copy-start | bytes 1880068
  0.7 18.9 %copy-start.1 = (bf16[544,544]{1,0:T(8,128)(2,1)S(1)}, bf16[544,544]{1,0:T(8,128)(2,1)}, u32[]{:S(2)}) copy-start(bf16[544,544]{1,0:T(8,128)(2,1)} %kernel_ref.1) | copy-start | bytes 1775620
  0.7 18.9 %copy-start.2 = (bf16[32,3,544]{2,0,1:T(8,128)(2,1)S(1)}, bf16[32,3,544]{2,0,1:T(8,128)(2,1)}, u32[]{:S(2)}) copy-start(bf16[32,3,544]{2,0,1:T(8,128)(2,1)} %param.12) | copy-start | bytes 313348
  0.7 18.9 %copy-start.3 = (bf16[32,544]{1,0:T(8,128)(2,1)S(1)}, bf16[32,544]{1,0:T(8,128)(2,1)}, u32[]{:S(2)}) copy-start(bf16[32,544]{1,0:T(8,128)(2,1)} %jac_ref.1) | copy-start | bytes 104452
  8.1 24.9 %copy-start.4 = (f32[4,3,3,128]{3,0,2,1:T(4,128)S(1)}, f32[4,3,3,128]{3,0,2,1:T(4,128)}, u32[]{:S(2)}) copy-start(f32[4,3,3,128]{3,0,2,1:T(4,128)} %param.23) | copy-start | bytes 55300
  8.1 28.0 %all-to-all-start = ((bf16[128,24,128]{2,1,0:T(8,128)(2,1)}), bf16[128,24,128]{2,1,0:T(8,128)(2,1)S(1)}, u32[]{:S(2)}, u32[]{:S(2)}) async-start(bf16[128,24,128]{2,1,0:T(8,128)(2,1)} %bitcast.14), calls=%async_computation | async-start | bytes 1572864 | tf_op jit(solution)/shard_map/all_to_all | solution.py:335
  21.0 8.4 %collective-permute-start = (f32[96,128]{1,0:T(8,128)S(1)}, f32[96,128]{1,0:T(8,128)S(1)}, u32[]{:S(2)}, u32[]{:S(2)}) collective-permute-start(f32[96,128]{1,0:T(8,128)S(1)} %get-tuple-element.17), channel_id=1, source_target_pairs={{0,1},{1,2},{2,3},{3,0},{4,5},{5,6},{6,7},{7,4},{8,9},{9,10},{10,1... | collective-permute-start | bytes 147464 | tf_op jit(solution)/shard_map/ppermute | solution.py:344
  22.5 10.4 %collective-permute-start.1 = (f32[96,128]{1,0:T(8,128)S(1)}, f32[96,128]{1,0:T(8,128)S(1)}, u32[]{:S(2)}, u32[]{:S(2)}) collective-permute-start(f32[96,128]{1,0:T(8,128)S(1)} %get-tuple-element.18), channel_id=1, source_target_pairs={{0,2},{1,3},{2,0},{3,1},{4,6},{5,7},{6,4},{7,5},{8,10},{9,11},{10,... | collective-permute-start | bytes 147464 | tf_op jit(solution)/shard_map/ppermute | solution.py:344
  24.9 8.0 %collective-permute-start.2 = (f32[96,128]{1,0:T(8,128)S(1)}, f32[96,128]{1,0:T(8,128)S(1)}, u32[]{:S(2)}, u32[]{:S(2)}) collective-permute-start(f32[96,128]{1,0:T(8,128)S(1)} %get-tuple-element.19), channel_id=1, source_target_pairs={{0,3},{1,0},{2,1},{3,2},{4,7},{5,4},{6,5},{7,6},{8,11},{9,8},{10,9... | collective-permute-start | bytes 147464 | tf_op jit(solution)/shard_map/ppermute | solution.py:344

commit v4 on v3

--- a/solution.py
+++ b/solution.py
@@ -103,13 +103,12 @@
     get_adj.wait()
     adj = adj_ref[...].reshape(comps * ves, points)
     even = points // 256 * 256
+    refined = 256 - (points - even)
 
     def project(start, stop):
         at = slice(start, stop)
-        body = down_ref[:even, at]
-        tail = down_ref[even:, at]
-        m = mm(high[:, :even], body) + mm(low[:, :even], body)
-        m_ref[:, at] = (m + mm(tails, jnp.concatenate([tail, tail], axis=0))).astype(jnp.bfloat16)
+        last = jnp.concatenate([down_ref[even:, at], down_ref[:refined, at]], axis=0)
+        m_ref[:, at] = (mm(high[:, :even], down_ref[:even, at]) + mm(tails, last)).astype(jnp.bfloat16)
 
     def fields(start, stop):
         for s in range(start, stop, LANES):
@@ -130,7 +129,7 @@
         if i == 0:
             get_analysis.wait()
             high, low = split(analysis_ref[...])
-            tails = jnp.concatenate([high[:, even:], low[:, even:]], axis=1)
+            tails = jnp.concatenate([high[:, even:], low[:, :refined]], axis=1)
         get_down[i].wait()
         for s in range(start, stop, 256):
             project(s, min(s + 256, stop))

time: 37.6 us -> 36.9 us (0.981)
  Pallas kernels: 10.2 us -> 9.53 us
    pallas_call x1, Pallas kernels: 7.35 us -> 6.7 us  [call_pairs(): pl.pallas_call(pairs_kernel, out_shape=jax.ShapeDtypeStruct(out, jnp.bflo...]
where the time goes in v4:
time: 36.9 us; the launch traced here: 36.7 us
  starting transfers between devices  16.5 us (45%)
  waiting for transfers between devices  9.88 us (27%)
  Pallas kernels  9.53 us (26%)
  between operations  0.75 us (2%)
    all_to_all x1, starting transfers between devices, body(): lax.all_to_all(sent.reshape(groups * ves_count, ROWS, LANES), ('deg', 've...  11.5 us
    ppermute x3, waiting for transfers between devices, body(): lax.ppermute(selfs[i], 'deg', [(j, (j + i) % groups) for j in range(group...  6.83 us
    pallas_call x1, Pallas kernels, call_pairs(): pl.pallas_call(pairs_kernel, out_shape=jax.ShapeDtypeStruct(out, jnp.bflo...  6.7 us
    ppermute x3, starting transfers between devices, body(): lax.ppermute(selfs[i], 'deg', [(j, (j + i) % groups) for j in range(group...  5.04 us
    all_to_all x1, waiting for transfers between devices, body(): lax.all_to_all(sent.reshape(groups * ves_count, ROWS, LANES), ('deg', 've...  3.05 us
    pallas_call x1, Pallas kernels, call_self(): pl.pallas_call(self_kernel_body, out_shape=[jax.ShapeDtypeStruct((comps *...  1.41 us
    pallas_call x1, Pallas kernels, call_solve(): pl.pallas_call(solve_kernel, out_shape=jax.ShapeDtypeStruct(prepared[0].s...  1.27 us
  transfers between devices with their start and end apart: 4, of which 3 were waited for; matrix products, arithmetic and copies ran while one was open for 0% of the time, Pallas kernels for 4%

profile of v4, /device:TPU:1, one launch (start us, length us, event | category | flops | bytes accessed | tf_op | source)
XLA Modules:
  0.0 36.7 jit_solution(2694673141283299864)
XLA Ops:
  0.7 0.0 copy-start
  0.7 0.0 copy-start.1
  0.7 0.0 copy-start.2
  0.7 0.0 copy-start.3
  0.7 6.7 %pairs.1 = bf16[4,768,128]{2,1,0:T(8,128)(2,1)} custom-call(s32[1]{0:T(128)S(6)} %copy.13.live_hbm, bf16[3,32,544]{2,1,0:T(8,128)(2,1)} %bitcast.11, bf16[544,2112]{1,0:T(8,128)(2,1)} %up_hbm.1, bf16[544,2112]{1,0:T(8,128)(2,1)} %bitcast.15, f32[2112]{0:T(1024)} %radial_hbm.1, f32[8,32]{1,0:T(8,128)} %bitcast.16, s32[8,32]{1,0:T(8,128)} %bitcast.17, ...), custom_call_target="tpu_custom_call" | custom-call | tf_op jit(solution)/shard_map/pairs/pallas_call | solution.py:163
  7.4 0.0 copy-start.4
  7.4 11.5 %all-to-all-start = ((bf16[128,24,128]{2,1,0:T(8,128)(2,1)}), bf16[128,24,128]{2,1,0:T(8,128)(2,1)S(1)}, u32[]{:S(2)}, u32[]{:S(2)}) async-start(bf16[128,24,128]{2,1,0:T(8,128)(2,1)} %bitcast.14), calls=%async_computation | async-start | bytes 1572864 | tf_op jit(solution)/shard_map/all_to_all | solution.py:334
  18.9 0.0 copy-done
  18.9 0.0 copy-done.1
  18.9 0.0 copy-done.2
  18.9 0.0 copy-done.3
  19.0 1.4 %self_term.1 = (f32[96,128]{1,0:T(8,128)S(1)}, f32[96,128]{1,0:T(8,128)S(1)}, f32[96,128]{1,0:T(8,128)S(1)}, f32[96,128]{1,0:T(8,128)S(1)}) custom-call(s32[1]{0:T(128)} %bitcast.6.group_ref, bf16[3,32,544]{2,1,0:T(8,128)(2,1)S(1)} %bitcast.12, bf16[32,544]{1,0:T(8,128)(2,1)S(1)} %copy-done.3, bf16[544,544]{1,0:T(8,128)(2,1)S(1)} %copy-done.1, ...), custom_call_target="tpu_custom_call" | custom-call | tf_op jit(solution)/shard_map/self_term/pallas_call | solution.py:205
  20.4 1.5 %collective-permute-start = (f32[96,128]{1,0:T(8,128)S(1)}, f32[96,128]{1,0:T(8,128)S(1)}, u32[]{:S(2)}, u32[]{:S(2)}) collective-permute-start(f32[96,128]{1,0:T(8,128)S(1)} %get-tuple-element.17), channel_id=1, source_target_pairs={{0,1},{1,2},{2,3},{3,0},{4,5},{5,6},{6,7},{7,4},{8,9},{9,10},{10,1... | collective-permute-start | bytes 147464 | tf_op jit(solution)/shard_map/ppermute | solution.py:343
  21.8 2.4 %collective-permute-start.1 = (f32[96,128]{1,0:T(8,128)S(1)}, f32[96,128]{1,0:T(8,128)S(1)}, u32[]{:S(2)}, u32[]{:S(2)}) collective-permute-start(f32[96,128]{1,0:T(8,128)S(1)} %get-tuple-element.18), channel_id=1, source_target_pairs={{0,2},{1,3},{2,0},{3,1},{4,6},{5,7},{6,4},{7,5},{8,10},{9,11},{10,... | collective-permute-start | bytes 147464 | tf_op jit(solution)/shard_map/ppermute | solution.py:343
  24.3 1.1 %collective-permute-start.2 = (f32[96,128]{1,0:T(8,128)S(1)}, f32[96,128]{1,0:T(8,128)S(1)}, u32[]{:S(2)}, u32[]{:S(2)}) collective-permute-start(f32[96,128]{1,0:T(8,128)S(1)} %get-tuple-element.19), channel_id=1, source_target_pairs={{0,3},{1,0},{2,1},{3,2},{4,7},{5,4},{6,5},{7,6},{8,11},{9,8},{10,9... | collective-permute-start | bytes 147464 | tf_op jit(solution)/shard_map/ppermute | solution.py:343
  25.4 3.3 %collective-permute-done.refs_1_ = f32[96,128]{1,0:T(8,128)S(1)} collective-permute-done((f32[96,128]{1,0:T(8,128)S(1)}, f32[96,128]{1,0:T(8,128)S(1)}, u32[]{:S(2)}, u32[]{:S(2)}) %collective-permute-start) | collective-permute-done | bytes 49184 | tf_op jit(solution)/shard_map/ppermute | solution.py:343
  28.7 3.5 %collective-permute-done.1.refs_2_ = f32[96,128]{1,0:T(8,128)S(1)} collective-permute-done((f32[96,128]{1,0:T(8,128)S(1)}, f32[96,128]{1,0:T(8,128)S(1)}, u32[]{:S(2)}, u32[]{:S(2)}) %collective-permute-start.1) | collective-permute-done | bytes 49184 | tf_op jit(solution)/shard_map/ppermute | solution.py:343
  32.2 0.0 collective-permute-done.2.refs_3_
  32.2 0.0 copy-done.4
  32.2 0.2 prepare.1
  32.4 3.0 %all-to-all-done.got_ref = bf16[128,24,128]{2,1,0:T(8,128)(2,1)S(1)} async-done(((bf16[128,24,128]{2,1,0:T(8,128)(2,1)}), bf16[128,24,128]{2,1,0:T(8,128)(2,1)S(1)}, u32[]{:S(2)}, u32[]{:S(2)}) %all-to-all-start) | async-done | bytes 786464 | tf_op jit(solution)/shard_map/all_to_all | solution.py:334
  35.5 1.3 %solve.1 = f32[3,72,128]{2,1,0:T(8,128)} custom-call(bf16[128,24,128]{2,1,0:T(8,128)(2,1)S(1)} %all-to-all-done.got_ref, f32[3,72,128]{2,1,0:T(8,128)S(1)} %get-tuple-element.20.self_ref, f32[3,3,72,128]{3,2,1,0:T(8,128)S(1)} %get-tuple-element.21.cofactor_ref, f32[72,128]{1,0:T(8,128)S(1)} %get-tuple-element.22.det_ref), custom_call_target="tpu_custom_call" | custom-call | tf_op jit(solution)/shard_map/solve/pallas_call | solution.py:301
Async XLA Ops:
  0.7 18.3 %copy-start = (f32[544,288]{0,1:T(8,128)S(1)}, f32[544,288]{0,1:T(8,128)}, u32[]{:S(2)}) copy-start(f32[544,288]{0,1:T(8,128)} %param.22) | copy-start | bytes 1880068
  0.7 18.3 %copy-start.1 = (bf16[544,544]{1,0:T(8,128)(2,1)S(1)}, bf16[544,544]{1,0:T(8,128)(2,1)}, u32[]{:S(2)}) copy-start(bf16[544,544]{1,0:T(8,128)(2,1)} %kernel_ref.1) | copy-start | bytes 1775620
  0.7 18.3 %copy-start.2 = (bf16[32,3,544]{2,0,1:T(8,128)(2,1)S(1)}, bf16[32,3,544]{2,0,1:T(8,128)(2,1)}, u32[]{:S(2)}) copy-start(bf16[32,3,544]{2,0,1:T(8,128)(2,1)} %param.12) | copy-start | bytes 313348
  0.7 18.3 %copy-start.3 = (bf16[32,544]{1,0:T(8,128)(2,1)S(1)}, bf16[32,544]{1,0:T(8,128)(2,1)}, u32[]{:S(2)}) copy-start(bf16[32,544]{1,0:T(8,128)(2,1)} %jac_ref.1) | copy-start | bytes 104452
  7.4 24.8 %copy-start.4 = (f32[4,3,3,128]{3,0,2,1:T(4,128)S(1)}, f32[4,3,3,128]{3,0,2,1:T(4,128)}, u32[]{:S(2)}) copy-start(f32[4,3,3,128]{3,0,2,1:T(4,128)} %param.23) | copy-start | bytes 55300
  7.4 28.0 %all-to-all-start = ((bf16[128,24,128]{2,1,0:T(8,128)(2,1)}), bf16[128,24,128]{2,1,0:T(8,128)(2,1)S(1)}, u32[]{:S(2)}, u32[]{:S(2)}) async-start(bf16[128,24,128]{2,1,0:T(8,128)(2,1)} %bitcast.14), calls=%async_computation | async-start | bytes 1572864 | tf_op jit(solution)/shard_map/all_to_all | solution.py:334
  20.4 8.4 %collective-permute-start = (f32[96,128]{1,0:T(8,128)S(1)}, f32[96,128]{1,0:T(8,128)S(1)}, u32[]{:S(2)}, u32[]{:S(2)}) collective-permute-start(f32[96,128]{1,0:T(8,128)S(1)} %get-tuple-element.17), channel_id=1, source_target_pairs={{0,1},{1,2},{2,3},{3,0},{4,5},{5,6},{6,7},{7,4},{8,9},{9,10},{10,1... | collective-permute-start | bytes 147464 | tf_op jit(solution)/shard_map/ppermute | solution.py:343
  21.8 10.4 %collective-permute-start.1 = (f32[96,128]{1,0:T(8,128)S(1)}, f32[96,128]{1,0:T(8,128)S(1)}, u32[]{:S(2)}, u32[]{:S(2)}) collective-permute-start(f32[96,128]{1,0:T(8,128)S(1)} %get-tuple-element.18), channel_id=1, source_target_pairs={{0,2},{1,3},{2,0},{3,1},{4,6},{5,7},{6,4},{7,5},{8,10},{9,11},{10,... | collective-permute-start | bytes 147464 | tf_op jit(solution)/shard_map/ppermute | solution.py:343
  24.3 8.0 %collective-permute-start.2 = (f32[96,128]{1,0:T(8,128)S(1)}, f32[96,128]{1,0:T(8,128)S(1)}, u32[]{:S(2)}, u32[]{:S(2)}) collective-permute-start(f32[96,128]{1,0:T(8,128)S(1)} %get-tuple-element.19), channel_id=1, source_target_pairs={{0,3},{1,0},{2,1},{3,2},{4,7},{5,4},{6,5},{7,6},{8,11},{9,8},{10,9... | collective-permute-start | bytes 147464 | tf_op jit(solution)/shard_map/ppermute | solution.py:343

commit v5 on v4

--- a/solution.py
+++ b/solution.py
@@ -179,8 +179,18 @@
     )(live, adj, up, down, radial, dist, owner, local, analysis)
 
 
-def self_kernel_body(group_ref, adj_ref, jac_ref, kernel_ref, analysis_ref, *refs):
-    *outs, s_ref = refs
+def self_kernel_body(group_ref, adj_hbm, jac_hbm, kernel_hbm, analysis_hbm, *refs):
+    *outs, adj_ref, jac_ref, kernel_ref, analysis_ref, s_ref, sem = refs
+    sources = [analysis_hbm, kernel_hbm, adj_hbm, jac_hbm]
+    targets = [analysis_ref, kernel_ref, adj_ref, jac_ref]
+    copies = [
+        pltpu.make_async_copy(source, target, sem.at[i])
+        for i, (source, target) in enumerate(zip(sources, targets))
+    ]
+    for copy in copies:
+        copy.start()
+    for copy in copies:
+        copy.wait()
     comps, ves, points = adj_ref.shape
     groups, wide, _ = s_ref.shape
     high, low = split(analysis_ref[...])
@@ -202,13 +212,18 @@
 def call_self(groups, group, adj, jac, kernel, analysis):
     comps, ves, points = adj.shape
     vmem = pl.BlockSpec(memory_space=pltpu.VMEM)
+    like = lambda a: pltpu.VMEM(a.shape, a.dtype)
     return pl.pallas_call(
         self_kernel_body,
         out_shape=[jax.ShapeDtypeStruct((comps * ves, LANES), jnp.float32)] * groups,
-        in_specs=[pl.BlockSpec(memory_space=pltpu.SMEM)] + [vmem] * 4,
+        in_specs=[pl.BlockSpec(memory_space=pltpu.SMEM)] + [pl.BlockSpec(memory_space=pl.ANY)] * 4,
         out_specs=[vmem] * groups,
-        scratch_shapes=[pltpu.VMEM((groups, analysis.shape[0] // groups, points), jnp.float32)],
-        compiler_params=pltpu.CompilerParams(vmem_limit_bytes=16 * 1024 * 1024),
+        scratch_shapes=[
+            like(adj), like(jac), like(kernel), like(analysis),
+            pltpu.VMEM((groups, analysis.shape[0] // groups, points), jnp.float32),
+            pltpu.SemaphoreType.DMA((4,)),
+        ],
+        compiler_params=pltpu.CompilerParams(vmem_limit_bytes=63 * 1024 * 1024),
         name="self_term",
     )(group, adj, jac, kernel, analysis)
 

time: 36.9 us -> 36.9 us (level)
  waiting for transfers between devices: 9.88 us -> 7.14 us
  Pallas kernels: 9.53 us -> 11.4 us
  local copies, waits for them, and re-layouts: 0.02 us -> 0.8 us
    pallas_call x1, Pallas kernels: 1.41 us -> 3.37 us  [call_self(): pl.pallas_call(self_kernel_body, out_shape=[jax.ShapeDtypeStruct((comps *...]
    all_to_all x1, waiting for transfers between devices: 3.05 us -> 1.15 us  [body(): lax.all_to_all(sent.reshape(groups * ves_count, ROWS, LANES), ('deg', 've...]
    ppermute x3, waiting for transfers between devices: 6.83 us -> 5.99 us  [body(): lax.ppermute(selfs[i], 'deg', [(j, (j + i) % groups) for j in range(group...]
    unnamed x10 -> x4, local copies, waits for them, and re-layouts: 0.02 us -> 0.8 us
  transfers between devices with their start and end apart: 4 -> 4, of which waited for: 3 -> 3; matrix products, arithmetic and copies ran while one was open for 0% -> 0% of each run, Pallas kernels for 4% -> 10%
where the time goes in v5:
time: 36.9 us; the launch traced here: 36.6 us
  starting transfers between devices  16.6 us (45%)
  Pallas kernels  11.4 us (31%)
  waiting for transfers between devices  7.14 us (19%)
  local copies, waits for them, and re-layouts  0.8 us (2%)
  between operations  0.69 us (2%)
    all_to_all x1, starting transfers between devices, body(): lax.all_to_all(sent.reshape(groups * ves_count, ROWS, LANES), ('deg', 've...  11.5 us
    pallas_call x1, Pallas kernels, call_pairs(): pl.pallas_call(pairs_kernel, out_shape=jax.ShapeDtypeStruct(out, jnp.bflo...  6.59 us
    ppermute x3, waiting for transfers between devices, body(): lax.ppermute(selfs[i], 'deg', [(j, (j + i) % groups) for j in range(group...  5.99 us
    ppermute x3, starting transfers between devices, body(): lax.ppermute(selfs[i], 'deg', [(j, (j + i) % groups) for j in range(group...  5.06 us
    pallas_call x1, Pallas kernels, call_self(): pl.pallas_call(self_kernel_body, out_shape=[jax.ShapeDtypeStruct((comps *...  3.37 us
    pallas_call x1, Pallas kernels, call_solve(): pl.pallas_call(solve_kernel, out_shape=jax.ShapeDtypeStruct(prepared[0].s...  1.26 us
    all_to_all x1, waiting for transfers between devices, body(): lax.all_to_all(sent.reshape(groups * ves_count, ROWS, LANES), ('deg', 've...  1.15 us
    unnamed x4, local copies, waits for them, and re-layouts  0.8 us
  transfers between devices with their start and end apart: 4, of which 3 were waited for; matrix products, arithmetic and copies ran while one was open for 0% of the time, Pallas kernels for 10%

profile of v5, /device:TPU:1, one launch (start us, length us, event | category | flops | bytes accessed | tf_op | source)
XLA Modules:
  0.0 36.6 jit_solution(17180856449219753534)
XLA Ops:
  0.7 6.6 %pairs.1 = bf16[4,768,128]{2,1,0:T(8,128)(2,1)} custom-call(s32[1]{0:T(128)S(6)} %copy.13.live_hbm, bf16[3,32,544]{2,1,0:T(8,128)(2,1)} %bitcast.14, bf16[544,2112]{1,0:T(8,128)(2,1)} %up_hbm.1, bf16[544,2112]{1,0:T(8,128)(2,1)} %bitcast.13, f32[2112]{0:T(1024)} %radial_hbm.1, f32[8,32]{1,0:T(8,128)} %bitcast.16, s32[8,32]{1,0:T(8,128)} %bitcast.17, ...), custom_call_target="tpu_custom_call" | custom-call | tf_op jit(solution)/shard_map/pairs/pallas_call | solution.py:163
  7.2 0.0 copy-start.1
  7.3 11.5 %all-to-all-start = ((bf16[128,24,128]{2,1,0:T(8,128)(2,1)}), bf16[128,24,128]{2,1,0:T(8,128)(2,1)S(1)}, u32[]{:S(2)}, u32[]{:S(2)}) async-start(bf16[128,24,128]{2,1,0:T(8,128)(2,1)} %bitcast.10), calls=%async_computation | async-start | bytes 1572864 | tf_op jit(solution)/shard_map/all_to_all | solution.py:349
  18.8 3.4 %self_term.1 = (f32[96,128]{1,0:T(8,128)}, f32[96,128]{1,0:T(8,128)}, f32[96,128]{1,0:T(8,128)}, f32[96,128]{1,0:T(8,128)}) custom-call(s32[1]{0:T(128)} %bitcast.6.group_ref, bf16[3,32,544]{2,1,0:T(8,128)(2,1)} %bitcast.15, bf16[32,544]{1,0:T(8,128)(2,1)} %jac_hbm.1, bf16[544,544]{1,0:T(8,128)(2,1)} %kernel_hbm.1, f32[288,544]{1,0:T(8,128)} %bitcast.12), custom_call_target="tpu_custom_call" | custom-call | tf_op jit(solution)/shard_map/self_term/pallas_call | solution.py:216
  22.1 1.5 %collective-permute-start = (f32[96,128]{1,0:T(8,128)}, f32[96,128]{1,0:T(8,128)S(1)}, u32[]{:S(2)}, u32[]{:S(2)}) collective-permute-start(f32[96,128]{1,0:T(8,128)} %get-tuple-element.17), channel_id=1, source_target_pairs={{0,1},{1,2},{2,3},{3,0},{4,5},{5,6},{6,7},{7,4},{8,9},{9,10},{10,1... | collective-permute-start | bytes 147464 | tf_op jit(solution)/shard_map/ppermute | solution.py:358
  23.6 2.4 %collective-permute-start.1 = (f32[96,128]{1,0:T(8,128)}, f32[96,128]{1,0:T(8,128)S(1)}, u32[]{:S(2)}, u32[]{:S(2)}) collective-permute-start(f32[96,128]{1,0:T(8,128)} %get-tuple-element.18), channel_id=1, source_target_pairs={{0,2},{1,3},{2,0},{3,1},{4,6},{5,7},{6,4},{7,5},{8,10},{9,11},{10,... | collective-permute-start | bytes 147464 | tf_op jit(solution)/shard_map/ppermute | solution.py:358
  26.1 1.1 %collective-permute-start.2 = (f32[96,128]{1,0:T(8,128)}, f32[96,128]{1,0:T(8,128)S(1)}, u32[]{:S(2)}, u32[]{:S(2)}) collective-permute-start(f32[96,128]{1,0:T(8,128)} %get-tuple-element.19), channel_id=1, source_target_pairs={{0,3},{1,0},{2,1},{3,2},{4,7},{5,4},{6,5},{7,6},{8,11},{9,8},{10,9... | collective-permute-start | bytes 147464 | tf_op jit(solution)/shard_map/ppermute | solution.py:358
  27.2 2.3 %collective-permute-done.refs_1_ = f32[96,128]{1,0:T(8,128)S(1)} collective-permute-done((f32[96,128]{1,0:T(8,128)}, f32[96,128]{1,0:T(8,128)S(1)}, u32[]{:S(2)}, u32[]{:S(2)}) %collective-permute-start) | collective-permute-done | bytes 49184 | tf_op jit(solution)/shard_map/ppermute | solution.py:358
  29.5 3.7 %collective-permute-done.1.refs_2_ = f32[96,128]{1,0:T(8,128)S(1)} collective-permute-done((f32[96,128]{1,0:T(8,128)}, f32[96,128]{1,0:T(8,128)S(1)}, u32[]{:S(2)}, u32[]{:S(2)}) %collective-permute-start.1) | collective-permute-done | bytes 49184 | tf_op jit(solution)/shard_map/ppermute | solution.py:358
  33.2 0.0 collective-permute-done.2.refs_3_
  33.2 0.0 copy-done.1
  33.2 0.0 copy-start
  33.2 0.8 %copy-done = f32[96,128]{1,0:T(8,128)S(1)} copy-done((f32[96,128]{1,0:T(8,128)S(1)}, f32[96,128]{1,0:T(8,128)}, u32[]{:S(2)}) %copy-start) | copy-done | bytes 49176
  34.0 0.2 prepare.1
  34.1 1.1 %all-to-all-done.got_ref = bf16[128,24,128]{2,1,0:T(8,128)(2,1)S(1)} async-done(((bf16[128,24,128]{2,1,0:T(8,128)(2,1)}), bf16[128,24,128]{2,1,0:T(8,128)(2,1)S(1)}, u32[]{:S(2)}, u32[]{:S(2)}) %all-to-all-start) | async-done | bytes 786464 | tf_op jit(solution)/shard_map/all_to_all | solution.py:349
  35.3 1.3 %solve.1 = f32[3,72,128]{2,1,0:T(8,128)} custom-call(bf16[128,24,128]{2,1,0:T(8,128)(2,1)S(1)} %all-to-all-done.got_ref, f32[3,72,128]{2,1,0:T(8,128)S(1)} %get-tuple-element.20.self_ref, f32[3,3,72,128]{3,2,1,0:T(8,128)S(1)} %get-tuple-element.21.cofactor_ref, f32[72,128]{1,0:T(8,128)S(1)} %get-tuple-element.22.det_ref), custom_call_target="tpu_custom_call" | custom-call | tf_op jit(solution)/shard_map/solve/pallas_call | solution.py:316
Async XLA Ops:
  7.2 25.9 %copy-start.1 = (f32[4,3,3,128]{3,0,2,1:T(4,128)S(1)}, f32[4,3,3,128]{3,0,2,1:T(4,128)}, u32[]{:S(2)}) copy-start(f32[4,3,3,128]{3,0,2,1:T(4,128)} %param.23) | copy-start | bytes 55300
  7.3 28.0 %all-to-all-start = ((bf16[128,24,128]{2,1,0:T(8,128)(2,1)}), bf16[128,24,128]{2,1,0:T(8,128)(2,1)S(1)}, u32[]{:S(2)}, u32[]{:S(2)}) async-start(bf16[128,24,128]{2,1,0:T(8,128)(2,1)} %bitcast.10), calls=%async_computation | async-start | bytes 1572864 | tf_op jit(solution)/shard_map/all_to_all | solution.py:349
  22.1 7.3 %collective-permute-start = (f32[96,128]{1,0:T(8,128)}, f32[96,128]{1,0:T(8,128)S(1)}, u32[]{:S(2)}, u32[]{:S(2)}) collective-permute-start(f32[96,128]{1,0:T(8,128)} %get-tuple-element.17), channel_id=1, source_target_pairs={{0,1},{1,2},{2,3},{3,0},{4,5},{5,6},{6,7},{7,4},{8,9},{9,10},{10,1... | collective-permute-start | bytes 147464 | tf_op jit(solution)/shard_map/ppermute | solution.py:358
  23.6 9.6 %collective-permute-start.1 = (f32[96,128]{1,0:T(8,128)}, f32[96,128]{1,0:T(8,128)S(1)}, u32[]{:S(2)}, u32[]{:S(2)}) collective-permute-start(f32[96,128]{1,0:T(8,128)} %get-tuple-element.18), channel_id=1, source_target_pairs={{0,2},{1,3},{2,0},{3,1},{4,6},{5,7},{6,4},{7,5},{8,10},{9,11},{10,... | collective-permute-start | bytes 147464 | tf_op jit(solution)/shard_map/ppermute | solution.py:358
  26.1 7.1 %collective-permute-start.2 = (f32[96,128]{1,0:T(8,128)}, f32[96,128]{1,0:T(8,128)S(1)}, u32[]{:S(2)}, u32[]{:S(2)}) collective-permute-start(f32[96,128]{1,0:T(8,128)} %get-tuple-element.19), channel_id=1, source_target_pairs={{0,3},{1,0},{2,1},{3,2},{4,7},{5,4},{6,5},{7,6},{8,11},{9,8},{10,9... | collective-permute-start | bytes 147464 | tf_op jit(solution)/shard_map/ppermute | solution.py:358
  33.2 0.8 %copy-start = (f32[96,128]{1,0:T(8,128)S(1)}, f32[96,128]{1,0:T(8,128)}, u32[]{:S(2)}) copy-start(f32[96,128]{1,0:T(8,128)} %get-tuple-element.16.refs_0_) | copy-start | bytes 147460

commit v6 on v5

--- a/solution.py
+++ b/solution.py
@@ -45,15 +45,16 @@
     place = mm(ones, (hot * (lane + 1).astype(jnp.float32)).astype(jnp.bfloat16), NT)
     ids = jnp.where(lane == 0, columns(ident.astype(jnp.float32), ves), 0.0)
     ids = mm(ones, ids.astype(jnp.bfloat16), NT)
-    slot = ((place - 1.0) * SLOTS + rank)[:1].astype(jnp.int32)
-    shape = (ves_count, ROWS, pairs)
-    row = lax.broadcasted_iota(jnp.int32, shape, 1)
-    base = lax.broadcasted_iota(jnp.int32, shape, 0) * SLOTS
+    slot = ((place - 1.0) * SLOTS + rank)[:1]
+    row = lax.broadcasted_iota(jnp.int32, (ROWS, pairs), 0)
     tile, inner = row // 8, row % 8
-    code = (base + jnp.where(tile == 2, 8 + inner % 4, inner)).reshape(-1, pairs)
-    upper = jnp.where(tile == 2, inner // 4, tile).reshape(-1, pairs)
-    match = code == slot
-    pick = [jnp.where(match & (upper == half), 1.0, 0.0) for half in range(2)]
+    code = jnp.where(tile == 2, 8 + inner % 4, inner).astype(jnp.float32)
+    upper = jnp.where(tile == 2, inner // 4, tile)
+    pick = []
+    for half in range(2):
+        wanted = jnp.where(upper == half, code, 1e6)
+        hits = [jnp.where(wanted == slot - k * SLOTS, 1.0, 0.0) for k in range(ves_count)]
+        pick.append(jnp.concatenate(hits, axis=0))
     return jnp.concatenate(pick, axis=1).astype(jnp.bfloat16), ids
 
 
@@ -215,7 +216,7 @@
     like = lambda a: pltpu.VMEM(a.shape, a.dtype)
     return pl.pallas_call(
         self_kernel_body,
-        out_shape=[jax.ShapeDtypeStruct((comps * ves, LANES), jnp.float32)] * groups,
+        out_shape=[pltpu.VMEM((comps * ves, LANES), jnp.float32)] * groups,
         in_specs=[pl.BlockSpec(memory_space=pltpu.SMEM)] + [pl.BlockSpec(memory_space=pl.ANY)] * 4,
         out_specs=[vmem] * groups,
         scratch_shapes=[

time: 36.9 us -> 36.8 us (level)
  waiting for transfers between devices: 7.14 us -> 7.83 us
  Pallas kernels: 11.4 us -> 10.8 us
    pallas_call x1, Pallas kernels: 3.37 us -> 2.78 us  [call_self(): pl.pallas_call(self_kernel_body, out_shape=[pltpu.VMEM((comps * ves, LANE...]
    all_to_all x1, waiting for transfers between devices: 1.15 us -> 1.61 us  [body(): lax.all_to_all(sent.reshape(groups * ves_count, ROWS, LANES), ('deg', 've...]
    unnamed x4 -> x2, local copies, waits for them, and re-layouts: 0.8 us -> 0.72 us
  transfers between devices with their start and end apart: 4 -> 4, of which waited for: 3 -> 3; matrix products, arithmetic and copies ran while one was open for 0% -> 0% of each run, Pallas kernels for 10% -> 8%
where the time goes in v6:
time: 36.8 us; the launch traced here: 36.5 us
  starting transfers between devices  16.5 us (45%)
  Pallas kernels  10.8 us (29%)
  waiting for transfers between devices  7.83 us (21%)
  local copies, waits for them, and re-layouts  0.72 us (2%)
  between operations  0.68 us (2%)
    all_to_all x1, starting transfers between devices, body(): lax.all_to_all(sent.reshape(groups * ves_count, ROWS, LANES), ('deg', 've...  11.5 us
    pallas_call x1, Pallas kernels, call_pairs(): pl.pallas_call(pairs_kernel, out_shape=jax.ShapeDtypeStruct(out, jnp.bflo...  6.58 us
    ppermute x3, waiting for transfers between devices, body(): lax.ppermute(selfs[i], 'deg', [(j, (j + i) % groups) for j in range(group...  6.22 us
    ppermute x3, starting transfers between devices, body(): lax.ppermute(selfs[i], 'deg', [(j, (j + i) % groups) for j in range(group...  5.04 us
    pallas_call x1, Pallas kernels, call_self(): pl.pallas_call(self_kernel_body, out_shape=[pltpu.VMEM((comps * ves, LANE...  2.78 us
    all_to_all x1, waiting for transfers between devices, body(): lax.all_to_all(sent.reshape(groups * ves_count, ROWS, LANES), ('deg', 've...  1.61 us
    pallas_call x1, Pallas kernels, call_solve(): pl.pallas_call(solve_kernel, out_shape=jax.ShapeDtypeStruct(prepared[0].s...  1.26 us
  transfers between devices with their start and end apart: 4, of which 3 were waited for; matrix products, arithmetic and copies ran while one was open for 0% of the time, Pallas kernels for 8%

profile of v6, /device:TPU:1, one launch (start us, length us, event | category | flops | bytes accessed | tf_op | source)
XLA Modules:
  0.0 36.5 jit_solution(6604838689820392725)
XLA Ops:
  0.7 6.6 %pairs.1 = bf16[4,768,128]{2,1,0:T(8,128)(2,1)} custom-call(s32[1]{0:T(128)S(6)} %copy.13.live_hbm, bf16[3,32,544]{2,1,0:T(8,128)(2,1)} %bitcast.14, bf16[544,2112]{1,0:T(8,128)(2,1)} %up_hbm.1, bf16[544,2112]{1,0:T(8,128)(2,1)} %bitcast.13, f32[2112]{0:T(1024)} %radial_hbm.1, f32[8,32]{1,0:T(8,128)} %bitcast.16, s32[8,32]{1,0:T(8,128)} %bitcast.17, ...), custom_call_target="tpu_custom_call" | custom-call | tf_op jit(solution)/shard_map/pairs/pallas_call | solution.py:164
  7.2 11.5 %all-to-all-start = ((bf16[128,24,128]{2,1,0:T(8,128)(2,1)}), bf16[128,24,128]{2,1,0:T(8,128)(2,1)S(1)}, u32[]{:S(2)}, u32[]{:S(2)}) async-start(bf16[128,24,128]{2,1,0:T(8,128)(2,1)} %bitcast.10), calls=%async_computation | async-start | bytes 1572864 | tf_op jit(solution)/shard_map/all_to_all | solution.py:350
  18.7 2.8 %self_term.1 = (f32[96,128]{1,0:T(8,128)S(1)}, f32[96,128]{1,0:T(8,128)S(1)}, f32[96,128]{1,0:T(8,128)S(1)}, f32[96,128]{1,0:T(8,128)S(1)}) custom-call(s32[1]{0:T(128)} %bitcast.6.group_ref, bf16[3,32,544]{2,1,0:T(8,128)(2,1)} %bitcast.15, bf16[32,544]{1,0:T(8,128)(2,1)} %jac_hbm.1, bf16[544,544]{1,0:T(8,128)(2,1)} %kernel_hbm.1, f32[288,544]{1,0:T(8,128)} %bitcast.12), custom_call_target="tpu_custom_call" | custom-call | tf_op jit(solution)/shard_map/self_term/pallas_call | solution.py:217
  21.5 1.5 %collective-permute-start = (f32[96,128]{1,0:T(8,128)S(1)}, f32[96,128]{1,0:T(8,128)S(1)}, u32[]{:S(2)}, u32[]{:S(2)}) collective-permute-start(f32[96,128]{1,0:T(8,128)S(1)} %get-tuple-element.17), channel_id=1, source_target_pairs={{0,1},{1,2},{2,3},{3,0},{4,5},{5,6},{6,7},{7,4},{8,9},{9,10},{10,1... | collective-permute-start | bytes 147464 | tf_op jit(solution)/shard_map/ppermute | solution.py:359
  23.0 2.4 %collective-permute-start.1 = (f32[96,128]{1,0:T(8,128)S(1)}, f32[96,128]{1,0:T(8,128)S(1)}, u32[]{:S(2)}, u32[]{:S(2)}) collective-permute-start(f32[96,128]{1,0:T(8,128)S(1)} %get-tuple-element.18), channel_id=1, source_target_pairs={{0,2},{1,3},{2,0},{3,1},{4,6},{5,7},{6,4},{7,5},{8,10},{9,11},{10,... | collective-permute-start | bytes 147464 | tf_op jit(solution)/shard_map/ppermute | solution.py:359
  25.4 1.1 %collective-permute-start.2 = (f32[96,128]{1,0:T(8,128)S(1)}, f32[96,128]{1,0:T(8,128)S(1)}, u32[]{:S(2)}, u32[]{:S(2)}) collective-permute-start(f32[96,128]{1,0:T(8,128)S(1)} %get-tuple-element.19), channel_id=1, source_target_pairs={{0,3},{1,0},{2,1},{3,2},{4,7},{5,4},{6,5},{7,6},{8,11},{9,8},{10,9... | collective-permute-start | bytes 147464 | tf_op jit(solution)/shard_map/ppermute | solution.py:359
  26.6 1.5 %collective-permute-done.refs_1_ = f32[96,128]{1,0:T(8,128)S(1)} collective-permute-done((f32[96,128]{1,0:T(8,128)S(1)}, f32[96,128]{1,0:T(8,128)S(1)}, u32[]{:S(2)}, u32[]{:S(2)}) %collective-permute-start) | collective-permute-done | bytes 49184 | tf_op jit(solution)/shard_map/ppermute | solution.py:359
  28.0 4.8 %collective-permute-done.1.refs_2_ = f32[96,128]{1,0:T(8,128)S(1)} collective-permute-done((f32[96,128]{1,0:T(8,128)S(1)}, f32[96,128]{1,0:T(8,128)S(1)}, u32[]{:S(2)}, u32[]{:S(2)}) %collective-permute-start.1) | collective-permute-done | bytes 49184 | tf_op jit(solution)/shard_map/ppermute | solution.py:359
  32.8 0.0 collective-permute-done.2.refs_3_
  32.8 0.0 copy-start
  32.8 0.7 %copy-done = f32[4,3,3,128]{3,0,2,1:T(4,128)S(1)} copy-done((f32[4,3,3,128]{3,0,2,1:T(4,128)S(1)}, f32[4,3,3,128]{3,0,2,1:T(4,128)}, u32[]{:S(2)}) %copy-start) | copy-done | bytes 18456
  33.5 0.2 prepare.1
  33.7 1.6 %all-to-all-done.got_ref = bf16[128,24,128]{2,1,0:T(8,128)(2,1)S(1)} async-done(((bf16[128,24,128]{2,1,0:T(8,128)(2,1)}), bf16[128,24,128]{2,1,0:T(8,128)(2,1)S(1)}, u32[]{:S(2)}, u32[]{:S(2)}) %all-to-all-start) | async-done | bytes 786464 | tf_op jit(solution)/shard_map/all_to_all | solution.py:350
  35.3 1.3 %solve.1 = f32[3,72,128]{2,1,0:T(8,128)} custom-call(bf16[128,24,128]{2,1,0:T(8,128)(2,1)S(1)} %all-to-all-done.got_ref, f32[3,72,128]{2,1,0:T(8,128)S(1)} %get-tuple-element.20.self_ref, f32[3,3,72,128]{3,2,1,0:T(8,128)S(1)} %get-tuple-element.21.cofactor_ref, f32[72,128]{1,0:T(8,128)S(1)} %get-tuple-element.22.det_ref), custom_call_target="tpu_custom_call" | custom-call | tf_op jit(solution)/shard_map/solve/pallas_call | solution.py:317
Async XLA Ops:
  7.2 28.0 %all-to-all-start = ((bf16[128,24,128]{2,1,0:T(8,128)(2,1)}), bf16[128,24,128]{2,1,0:T(8,128)(2,1)S(1)}, u32[]{:S(2)}, u32[]{:S(2)}) async-start(bf16[128,24,128]{2,1,0:T(8,128)(2,1)} %bitcast.10), calls=%async_computation | async-start | bytes 1572864 | tf_op jit(solution)/shard_map/all_to_all | solution.py:350
  21.5 6.5 %collective-permute-start = (f32[96,128]{1,0:T(8,128)S(1)}, f32[96,128]{1,0:T(8,128)S(1)}, u32[]{:S(2)}, u32[]{:S(2)}) collective-permute-start(f32[96,128]{1,0:T(8,128)S(1)} %get-tuple-element.17), channel_id=1, source_target_pairs={{0,1},{1,2},{2,3},{3,0},{4,5},{5,6},{6,7},{7,4},{8,9},{9,10},{10,1... | collective-permute-start | bytes 147464 | tf_op jit(solution)/shard_map/ppermute | solution.py:359
  23.0 9.8 %collective-permute-start.1 = (f32[96,128]{1,0:T(8,128)S(1)}, f32[96,128]{1,0:T(8,128)S(1)}, u32[]{:S(2)}, u32[]{:S(2)}) collective-permute-start(f32[96,128]{1,0:T(8,128)S(1)} %get-tuple-element.18), channel_id=1, source_target_pairs={{0,2},{1,3},{2,0},{3,1},{4,6},{5,7},{6,4},{7,5},{8,10},{9,11},{10,... | collective-permute-start | bytes 147464 | tf_op jit(solution)/shard_map/ppermute | solution.py:359
  25.4 7.4 %collective-permute-start.2 = (f32[96,128]{1,0:T(8,128)S(1)}, f32[96,128]{1,0:T(8,128)S(1)}, u32[]{:S(2)}, u32[]{:S(2)}) collective-permute-start(f32[96,128]{1,0:T(8,128)S(1)} %get-tuple-element.19), channel_id=1, source_target_pairs={{0,3},{1,0},{2,1},{3,2},{4,7},{5,4},{6,5},{7,6},{8,11},{9,8},{10,9... | collective-permute-start | bytes 147464 | tf_op jit(solution)/shard_map/ppermute | solution.py:359
  32.8 0.7 %copy-start = (f32[4,3,3,128]{3,0,2,1:T(4,128)S(1)}, f32[4,3,3,128]{3,0,2,1:T(4,128)}, u32[]{:S(2)}) copy-start(f32[4,3,3,128]{3,0,2,1:T(4,128)} %param.23) | copy-start | bytes 55300

commit v7 on v6

--- a/solution.py
+++ b/solution.py
@@ -133,8 +133,8 @@
             tails = jnp.concatenate([high[:, even:], low[:, :refined]], axis=1)
         get_down[i].wait()
         for s in range(start, stop, 256):
+            fields(s, min(s + 256, stop))
             project(s, min(s + 256, stop))
-            fields(s, min(s + 256, stop))
     part = mm(m_ref[...], field_ref[...], NT)
 
     zeros = jnp.zeros((2 * LANES - 3 * wide - 8, pairs), jnp.float32)

time: 36.8 us -> 36.8 us (level)
  no operation moved by 1% of the time
where the time goes in v7:
time: 36.8 us; the launch traced here: 36.5 us
  starting transfers between devices  16.5 us (45%)
  Pallas kernels  10.8 us (29%)
  waiting for transfers between devices  7.83 us (21%)
  local copies, waits for them, and re-layouts  0.72 us (2%)
  between operations  0.68 us (2%)
    all_to_all x1, starting transfers between devices, body(): lax.all_to_all(sent.reshape(groups * ves_count, ROWS, LANES), ('deg', 've...  11.5 us
    pallas_call x1, Pallas kernels, call_pairs(): pl.pallas_call(pairs_kernel, out_shape=jax.ShapeDtypeStruct(out, jnp.bflo...  6.58 us
    ppermute x3, waiting for transfers between devices, body(): lax.ppermute(selfs[i], 'deg', [(j, (j + i) % groups) for j in range(group...  6.22 us
    ppermute x3, starting transfers between devices, body(): lax.ppermute(selfs[i], 'deg', [(j, (j + i) % groups) for j in range(group...  5.04 us
    pallas_call x1, Pallas kernels, call_self(): pl.pallas_call(self_kernel_body, out_shape=[pltpu.VMEM((comps * ves, LANE...  2.78 us
    all_to_all x1, waiting for transfers between devices, body(): lax.all_to_all(sent.reshape(groups * ves_count, ROWS, LANES), ('deg', 've...  1.61 us
    pallas_call x1, Pallas kernels, call_solve(): pl.pallas_call(solve_kernel, out_shape=jax.ShapeDtypeStruct(prepared[0].s...  1.26 us
  transfers between devices with their start and end apart: 4, of which 3 were waited for; matrix products, arithmetic and copies ran while one was open for 0% of the time, Pallas kernels for 8%

profile of v7, /device:TPU:1, one launch (start us, length us, event | category | flops | bytes accessed | tf_op | source)
XLA Modules:
  0.0 36.5 jit_solution(6604838689820392725)
XLA Ops:
  0.7 6.6 %pairs.1 = bf16[4,768,128]{2,1,0:T(8,128)(2,1)} custom-call(s32[1]{0:T(128)S(6)} %copy.13.live_hbm, bf16[3,32,544]{2,1,0:T(8,128)(2,1)} %bitcast.14, bf16[544,2112]{1,0:T(8,128)(2,1)} %up_hbm.1, bf16[544,2112]{1,0:T(8,128)(2,1)} %bitcast.13, f32[2112]{0:T(1024)} %radial_hbm.1, f32[8,32]{1,0:T(8,128)} %bitcast.16, s32[8,32]{1,0:T(8,128)} %bitcast.17, ...), custom_call_target="tpu_custom_call" | custom-call | tf_op jit(solution)/shard_map/pairs/pallas_call | solution.py:164
  7.2 11.5 %all-to-all-start = ((bf16[128,24,128]{2,1,0:T(8,128)(2,1)}), bf16[128,24,128]{2,1,0:T(8,128)(2,1)S(1)}, u32[]{:S(2)}, u32[]{:S(2)}) async-start(bf16[128,24,128]{2,1,0:T(8,128)(2,1)} %bitcast.10), calls=%async_computation | async-start | bytes 1572864 | tf_op jit(solution)/shard_map/all_to_all | solution.py:350
  18.7 2.8 %self_term.1 = (f32[96,128]{1,0:T(8,128)S(1)}, f32[96,128]{1,0:T(8,128)S(1)}, f32[96,128]{1,0:T(8,128)S(1)}, f32[96,128]{1,0:T(8,128)S(1)}) custom-call(s32[1]{0:T(128)} %bitcast.6.group_ref, bf16[3,32,544]{2,1,0:T(8,128)(2,1)} %bitcast.15, bf16[32,544]{1,0:T(8,128)(2,1)} %jac_hbm.1, bf16[544,544]{1,0:T(8,128)(2,1)} %kernel_hbm.1, f32[288,544]{1,0:T(8,128)} %bitcast.12), custom_call_target="tpu_custom_call" | custom-call | tf_op jit(solution)/shard_map/self_term/pallas_call | solution.py:217
  21.5 1.5 %collective-permute-start = (f32[96,128]{1,0:T(8,128)S(1)}, f32[96,128]{1,0:T(8,128)S(1)}, u32[]{:S(2)}, u32[]{:S(2)}) collective-permute-start(f32[96,128]{1,0:T(8,128)S(1)} %get-tuple-element.17), channel_id=1, source_target_pairs={{0,1},{1,2},{2,3},{3,0},{4,5},{5,6},{6,7},{7,4},{8,9},{9,10},{10,1... | collective-permute-start | bytes 147464 | tf_op jit(solution)/shard_map/ppermute | solution.py:359
  23.0 2.4 %collective-permute-start.1 = (f32[96,128]{1,0:T(8,128)S(1)}, f32[96,128]{1,0:T(8,128)S(1)}, u32[]{:S(2)}, u32[]{:S(2)}) collective-permute-start(f32[96,128]{1,0:T(8,128)S(1)} %get-tuple-element.18), channel_id=1, source_target_pairs={{0,2},{1,3},{2,0},{3,1},{4,6},{5,7},{6,4},{7,5},{8,10},{9,11},{10,... | collective-permute-start | bytes 147464 | tf_op jit(solution)/shard_map/ppermute | solution.py:359
  25.4 1.1 %collective-permute-start.2 = (f32[96,128]{1,0:T(8,128)S(1)}, f32[96,128]{1,0:T(8,128)S(1)}, u32[]{:S(2)}, u32[]{:S(2)}) collective-permute-start(f32[96,128]{1,0:T(8,128)S(1)} %get-tuple-element.19), channel_id=1, source_target_pairs={{0,3},{1,0},{2,1},{3,2},{4,7},{5,4},{6,5},{7,6},{8,11},{9,8},{10,9... | collective-permute-start | bytes 147464 | tf_op jit(solution)/shard_map/ppermute | solution.py:359
  26.6 1.5 %collective-permute-done.refs_1_ = f32[96,128]{1,0:T(8,128)S(1)} collective-permute-done((f32[96,128]{1,0:T(8,128)S(1)}, f32[96,128]{1,0:T(8,128)S(1)}, u32[]{:S(2)}, u32[]{:S(2)}) %collective-permute-start) | collective-permute-done | bytes 49184 | tf_op jit(solution)/shard_map/ppermute | solution.py:359
  28.0 4.8 %collective-permute-done.1.refs_2_ = f32[96,128]{1,0:T(8,128)S(1)} collective-permute-done((f32[96,128]{1,0:T(8,128)S(1)}, f32[96,128]{1,0:T(8,128)S(1)}, u32[]{:S(2)}, u32[]{:S(2)}) %collective-permute-start.1) | collective-permute-done | bytes 49184 | tf_op jit(solution)/shard_map/ppermute | solution.py:359
  32.8 0.0 collective-permute-done.2.refs_3_
  32.8 0.0 copy-start
  32.8 0.7 %copy-done = f32[4,3,3,128]{3,0,2,1:T(4,128)S(1)} copy-done((f32[4,3,3,128]{3,0,2,1:T(4,128)S(1)}, f32[4,3,3,128]{3,0,2,1:T(4,128)}, u32[]{:S(2)}) %copy-start) | copy-done | bytes 18456
  33.5 0.2 prepare.1
  33.7 1.6 %all-to-all-done.got_ref = bf16[128,24,128]{2,1,0:T(8,128)(2,1)S(1)} async-done(((bf16[128,24,128]{2,1,0:T(8,128)(2,1)}), bf16[128,24,128]{2,1,0:T(8,128)(2,1)S(1)}, u32[]{:S(2)}, u32[]{:S(2)}) %all-to-all-start) | async-done | bytes 786464 | tf_op jit(solution)/shard_map/all_to_all | solution.py:350
  35.3 1.3 %solve.1 = f32[3,72,128]{2,1,0:T(8,128)} custom-call(bf16[128,24,128]{2,1,0:T(8,128)(2,1)S(1)} %all-to-all-done.got_ref, f32[3,72,128]{2,1,0:T(8,128)S(1)} %get-tuple-element.20.self_ref, f32[3,3,72,128]{3,2,1,0:T(8,128)S(1)} %get-tuple-element.21.cofactor_ref, f32[72,128]{1,0:T(8,128)S(1)} %get-tuple-element.22.det_ref), custom_call_target="tpu_custom_call" | custom-call | tf_op jit(solution)/shard_map/solve/pallas_call | solution.py:317
Async XLA Ops:
  7.2 28.0 %all-to-all-start = ((bf16[128,24,128]{2,1,0:T(8,128)(2,1)}), bf16[128,24,128]{2,1,0:T(8,128)(2,1)S(1)}, u32[]{:S(2)}, u32[]{:S(2)}) async-start(bf16[128,24,128]{2,1,0:T(8,128)(2,1)} %bitcast.10), calls=%async_computation | async-start | bytes 1572864 | tf_op jit(solution)/shard_map/all_to_all | solution.py:350
  21.5 6.5 %collective-permute-start = (f32[96,128]{1,0:T(8,128)S(1)}, f32[96,128]{1,0:T(8,128)S(1)}, u32[]{:S(2)}, u32[]{:S(2)}) collective-permute-start(f32[96,128]{1,0:T(8,128)S(1)} %get-tuple-element.17), channel_id=1, source_target_pairs={{0,1},{1,2},{2,3},{3,0},{4,5},{5,6},{6,7},{7,4},{8,9},{9,10},{10,1... | collective-permute-start | bytes 147464 | tf_op jit(solution)/shard_map/ppermute | solution.py:359
  23.0 9.8 %collective-permute-start.1 = (f32[96,128]{1,0:T(8,128)S(1)}, f32[96,128]{1,0:T(8,128)S(1)}, u32[]{:S(2)}, u32[]{:S(2)}) collective-permute-start(f32[96,128]{1,0:T(8,128)S(1)} %get-tuple-element.18), channel_id=1, source_target_pairs={{0,2},{1,3},{2,0},{3,1},{4,6},{5,7},{6,4},{7,5},{8,10},{9,11},{10,... | collective-permute-start | bytes 147464 | tf_op jit(solution)/shard_map/ppermute | solution.py:359
  25.4 7.4 %collective-permute-start.2 = (f32[96,128]{1,0:T(8,128)S(1)}, f32[96,128]{1,0:T(8,128)S(1)}, u32[]{:S(2)}, u32[]{:S(2)}) collective-permute-start(f32[96,128]{1,0:T(8,128)S(1)} %get-tuple-element.19), channel_id=1, source_target_pairs={{0,3},{1,0},{2,1},{3,2},{4,7},{5,4},{6,5},{7,6},{8,11},{9,8},{10,9... | collective-permute-start | bytes 147464 | tf_op jit(solution)/shard_map/ppermute | solution.py:359
  32.8 0.7 %copy-start = (f32[4,3,3,128]{3,0,2,1:T(4,128)S(1)}, f32[4,3,3,128]{3,0,2,1:T(4,128)}, u32[]{:S(2)}) copy-start(f32[4,3,3,128]{3,0,2,1:T(4,128)} %param.23) | copy-start | bytes 55300
